TPU v7x, 128 devices: a whole 4x4x4 slice. The times are simulated.
128 devices in a mesh: pipe: 2 (over core), ctx: 16 (over y, x), dp: 4 (over z).
Axes of the slice: x: 4, y: 4, z: 4, core: 2. Of those that a mesh axis runs over, the one named last changes fastest.
Arguments:
- queries: bfloat16 [2, 4, 2048, 2048], P('pipe', 'dp', 'ctx'), may hold values from -16 to 16
- key_rows: bfloat16 [2, 4, 2048, 512], P('pipe', 'dp', 'ctx'), may hold values from -8 to 8
- layer_value_rows: bfloat16 [2, 4, 2048, 512], P('pipe', 'dp', 'ctx'), may hold values from -6 to 6
- prior_output: bfloat16 [2, 4, 2048, 2048], P('pipe', 'dp', 'ctx'), may hold values from -3 to 3
- later_grad: bfloat16 [2, 4, 2048, 2048], P('pipe', 'dp', 'ctx'), may hold values from -6 to 6
- block_order: int32 [32], replicated, may hold values from 0 to 31, each once
- log_table: float32 [2, 16], P('pipe'), may hold values from 0 to 3
- dim_index: int32 [2, 64], P('pipe'), may hold values from 0 to 15, as said below
Outputs:
- attended: bfloat16 [2, 4, 2048, 2048], P('pipe', 'dp', 'ctx')
- query_gradient: bfloat16 [2, 4, 2048, 2048], P('pipe', 'dp', 'ctx')
- key_gradient: bfloat16 [2, 4, 2048, 512], P('pipe', 'dp', 'ctx')
- value_gradient: bfloat16 [2, 4, 2048, 512], P('pipe', 'dp', 'ctx')
- table_grad: float32 [2, 16], P('pipe')
Inputs may be any that keep to these rules, and one draw needn't show every extreme that they name: `block_order`: a permutation. `dim_index`: each row names every table entry equally often.
All inputs are finite; a program needn't handle non-finite values.
Results may differ from a plain program's by a relative error of at most 0.025.
Values may be sent and summed in bfloat16 or wider, within the bound.
No kernel may reach another device: no remote copies, remote signals or barrier semaphores. Data moves between devices by JAX's collectives and lax.ppermute only.
A program may use at most 64 MiB of HBM per device.

v0:
```python
import jax
import jax.numpy as jnp
from jax import lax
from jax.sharding import PartitionSpec as P

HEAD_SIZE = 128
neg_large = -1e30
rope_base = 500000.0


def passed_along(value, axis, by):
    size = lax.axis_size(axis)
    return lax.ppermute(value, axis, [(i, (i + by) % size) for i in range(size)])


def apply_rotation(vectors, cosine_values, sine_lookup):
    half_len = vectors.shape[-1] // 2
    lower_half = vectors[..., :half_len]
    upper_half = vectors[..., half_len:]
    return jnp.concatenate(
        [
            lower_half * cosine_values - upper_half * sine_lookup,
            lower_half * sine_lookup + upper_half * cosine_values,
        ],
        axis=-1,
    )


def rotate_back(gradient, cosine_values, sine_lookup):
    half_len = gradient.shape[-1] // 2
    lower_half = gradient[..., :half_len]
    upper_half = gradient[..., half_len:]
    return jnp.concatenate(
        [
            lower_half * cosine_values + upper_half * sine_lookup,
            upper_half * cosine_values - lower_half * sine_lookup,
        ],
        axis=-1,
    )


def angle_grad(gradient, rotated):
    half_len = gradient.shape[-1] // 2
    return jnp.sum(
        gradient[..., half_len:] * rotated[..., :half_len]
        - gradient[..., :half_len] * rotated[..., half_len:],
        axis=1,
    )


def angles_for(table_row, index_row, positions, head_dim):
    half_len = head_dim // 2
    onehot = (
        index_row[:, None] == jnp.arange(table_row.shape[0], dtype=jnp.int32)[None, :]
    ).astype(jnp.float32)
    log_factor = jnp.dot(onehot, table_row, precision=lax.Precision.HIGHEST)
    base_rate = rope_base ** (-(jnp.arange(half_len, dtype=jnp.float32) * 2.0 / head_dim))
    scaled_rate = base_rate * jnp.exp(-log_factor)
    return (onehot, positions[:, None] * scaled_rate[None, :])


def slot_positions(block_order, device, tok_rows):
    half_len = tok_rows // 2
    blocks = lax.dynamic_slice_in_dim(block_order, device * 2, 2)
    return (
        (blocks[:, None] * half_len + jnp.arange(half_len, dtype=jnp.int32)[None, :])
        .reshape(-1)
        .astype(jnp.float32)
    )


def on_device(
    queries, key_rows, layer_value_rows, prior_output, later_grad, block_order, log_table, dim_index
):
    tok_rows = queries.shape[2]
    q_width = queries.shape[3]
    kv_width = key_rows.shape[3]
    kv_heads = kv_width // HEAD_SIZE
    group_size = q_width // kv_width
    cycle_size = lax.axis_size("ctx")
    my_index = lax.axis_index("ctx")
    score_scale = HEAD_SIZE ** (-0.5)
    arriving = passed_along(prior_output, "pipe", 1)
    returning = passed_along(later_grad, "pipe", -1)
    positions = slot_positions(block_order, my_index, tok_rows)
    onehot, angles = angles_for(log_table[0], dim_index[0], positions, HEAD_SIZE)
    cosine_values = jnp.cos(angles)[:, None, :]
    sine_lookup = jnp.sin(angles)[:, None, :]
    mixed = (queries[0, 0].astype(jnp.float32) + arriving[0, 0].astype(jnp.float32)).reshape(
        tok_rows, kv_heads * group_size, HEAD_SIZE
    )
    rotated_query_rows = apply_rotation(mixed, cosine_values, sine_lookup).astype(jnp.bfloat16)
    rotated_key_rows = apply_rotation(
        key_rows[0, 0].astype(jnp.float32).reshape(tok_rows, kv_heads, HEAD_SIZE),
        cosine_values,
        sine_lookup,
    ).astype(jnp.bfloat16)
    grouped_queries = rotated_query_rows.reshape(tok_rows, kv_heads, group_size, HEAD_SIZE)
    value_head_rows = layer_value_rows[0, 0].reshape(tok_rows, kv_heads, HEAD_SIZE)
    output_gradient = returning[0, 0].reshape(tok_rows, kv_heads, group_size, HEAD_SIZE)
    key_value = jnp.stack([rotated_key_rows, value_head_rows])

    def visit(softmax_state, block_pair, key_pos):
        maxima, totals, accumulated = softmax_state
        scores = (
            jnp.einsum(
                "qhgd,khd->hgqk", grouped_queries, block_pair[0], preferred_element_type=jnp.float32
            )
            * score_scale
        )
        visible = key_pos[None, :] <= positions[:, None]
        row_max = jnp.max(jnp.where(visible, scores, neg_large), axis=-1)
        new_max = jnp.maximum(maxima, row_max)
        weights = jnp.where(visible, jnp.exp(scores - new_max[..., None]), 0.0)
        rescale = jnp.exp(maxima - new_max)
        totals = totals * rescale + jnp.sum(weights, axis=-1)
        summed = jnp.einsum(
            "hgqk,khd->qhgd",
            weights.astype(jnp.bfloat16),
            block_pair[1],
            preferred_element_type=jnp.float32,
        )
        accumulated = accumulated * jnp.moveaxis(rescale, -1, 0)[..., None] + summed
        return (new_max, totals, accumulated)

    def visit_back(block_pair, key_pos, log_totals, row_delta):
        scores = (
            jnp.einsum(
                "qhgd,khd->hgqk", grouped_queries, block_pair[0], preferred_element_type=jnp.float32
            )
            * score_scale
        )
        visible = key_pos[None, :] <= positions[:, None]
        probs = jnp.where(visible, jnp.exp(scores - log_totals[..., None]), 0.0)
        value_part = jnp.einsum(
            "hgqk,qhgd->khd",
            probs.astype(jnp.bfloat16),
            output_gradient,
            preferred_element_type=jnp.float32,
        )
        prob_grad = jnp.einsum(
            "qhgd,khd->hgqk", output_gradient, block_pair[1], preferred_element_type=jnp.float32
        )
        score_grad = (probs * (prob_grad - row_delta[..., None])).astype(jnp.bfloat16)
        query_part = jnp.einsum(
            "hgqk,khd->qhgd", score_grad, block_pair[0], preferred_element_type=jnp.float32
        )
        key_part = jnp.einsum(
            "hgqk,qhgd->khd", score_grad, grouped_queries, preferred_element_type=jnp.float32
        )
        return (query_part, jnp.stack([key_part, value_part]))

    initial = (
        jnp.full((kv_heads, group_size, tok_rows), neg_large, jnp.float32),
        jnp.zeros((kv_heads, group_size, tok_rows), jnp.float32),
        jnp.zeros((tok_rows, kv_heads, group_size, HEAD_SIZE), jnp.float32),
    )

    def guarded(softmax_state, block_pair, key_pos):
        return lax.cond(
            jnp.min(key_pos) <= jnp.max(positions),
            lambda held: visit(held, block_pair, key_pos),
            lambda held: held,
            softmax_state,
        )

    empty_query = jnp.zeros((tok_rows, kv_heads, group_size, HEAD_SIZE), jnp.float32)
    empty_pair = jnp.zeros((2, tok_rows, kv_heads, HEAD_SIZE), jnp.float32)

    def back_terms(block_pair, key_pos, log_totals, row_delta):
        return lax.cond(
            jnp.min(key_pos) <= jnp.max(positions),
            lambda held: visit_back(held, key_pos, log_totals, row_delta),
            lambda held: (empty_query, empty_pair),
            block_pair,
        )

    def forward_turn(turn_index, carried):
        softmax_state, block_pair = carried
        source = (my_index - turn_index) % cycle_size
        softmax_state = guarded(
            softmax_state, block_pair, slot_positions(block_order, source, tok_rows)
        )
        block_pair = passed_along(block_pair, "ctx", 1)
        return (softmax_state, block_pair)

    softmax_state, block_pair = lax.fori_loop(0, cycle_size - 1, forward_turn, (initial, key_value))
    last_source = (my_index + 1) % cycle_size
    softmax_state = guarded(
        softmax_state, block_pair, slot_positions(block_order, last_source, tok_rows)
    )
    maxima, totals, accumulated = softmax_state
    final_result = (accumulated / jnp.moveaxis(totals, -1, 0)[..., None]).astype(jnp.bfloat16)
    finish_log_totals = maxima + jnp.log(totals)
    finish_row_delta = jnp.moveaxis(
        jnp.sum(output_gradient.astype(jnp.float32) * final_result.astype(jnp.float32), axis=-1),
        0,
        -1,
    )
    final_result, log_totals, row_delta = (final_result, finish_log_totals, finish_row_delta)

    def backward_turn(turn_index, carried):
        query_sum, block_pair, travel_grads = carried
        source = (my_index - turn_index) % cycle_size
        key_pos = slot_positions(block_order, source, tok_rows)
        query_part, pair_part = back_terms(block_pair, key_pos, log_totals, row_delta)
        query_sum = query_sum + query_part
        travel_grads = travel_grads + pair_part
        block_pair = passed_along(block_pair, "ctx", 1)
        travel_grads = passed_along(travel_grads.astype(jnp.bfloat16), "ctx", 1).astype(
            travel_grads.dtype
        )
        return (query_sum, block_pair, travel_grads)

    query_sum, block_pair, own_grads = lax.fori_loop(
        0, cycle_size, backward_turn, (empty_query, key_value, empty_pair)
    )
    query_rot_grad = (query_sum * score_scale).reshape(tok_rows, kv_heads * group_size, HEAD_SIZE)
    key_rot_grad = own_grads[0] * score_scale
    query_gradient = rotate_back(query_rot_grad, cosine_values, sine_lookup).astype(jnp.bfloat16)
    key_gradient = rotate_back(key_rot_grad, cosine_values, sine_lookup).astype(jnp.bfloat16)
    value_gradient = own_grads[1].astype(jnp.bfloat16)
    angle_sums = angle_grad(query_rot_grad, rotated_query_rows.astype(jnp.float32)) + angle_grad(
        key_rot_grad, rotated_key_rows.astype(jnp.float32)
    )
    log_gradient = -jnp.sum(angle_sums * angles, axis=0)
    partial_value = jnp.dot(log_gradient, onehot, precision=lax.Precision.HIGHEST)
    summed_table = lax.psum(partial_value, ("ctx", "dp"))
    table_grad = summed_table / (cycle_size * lax.axis_size("dp") * tok_rows)
    return (
        final_result.reshape(1, 1, tok_rows, q_width),
        query_gradient.reshape(1, 1, tok_rows, q_width),
        key_gradient.reshape(1, 1, tok_rows, kv_width),
        value_gradient.reshape(1, 1, tok_rows, kv_width),
        table_grad[None, :],
    )


def solution(mesh):
    placed = (
        P("pipe", "dp", "ctx", None),
        P("pipe", "dp", "ctx", None),
        P("pipe", "dp", "ctx", None),
        P("pipe", "dp", "ctx", None),
        P("pipe", "dp", "ctx", None),
        P(),
        P("pipe", None),
        P("pipe", None),
    )
    return jax.shard_map(
        on_device,
        mesh=mesh,
        in_specs=placed,
        out_specs=(
            P("pipe", "dp", "ctx", None),
            P("pipe", "dp", "ctx", None),
            P("pipe", "dp", "ctx", None),
            P("pipe", "dp", "ctx", None),
            P("pipe", None),
        ),
        check_vma=False,
    )
```

profile of v0, /device:TPU:0, one launch (start us, length us, event | category | flops | bytes accessed | tf_op | source)
XLA Modules:
  0.0 693.5 jit_solution(15029671179001092386)
XLA Ops:
  14.0 171.1 %while.42 = (s32[]{:T(128)}, f32[4,4,128]{2,1,0:T(4,128)S(1)}, f32[4,4,128]{2,1,0:T(4,128)S(1)}, f32[128,4,4,128]{3,0,2,1:T(8,128)S(1)}, bf16[2,128,4,128]{3,1,2...) while((s32[]{:T(128)}, f32[4,4,128]{2,1,0:T(4,128)S(1)}, ...), condition=%wide.region_8.9_spmd.clone, body=%wide.region_2.8_spmd.clone.sunk | while | flops 137124752 | bytes 7803410 | solution.py:187
  18.4 3.3 conditional.8
  21.7 5.0 collective-permute-done
  29.5 3.3 conditional.8
  32.8 5.8 collective-permute-done
  41.4 3.3 conditional.8
  44.7 4.8 collective-permute-done
  52.4 7.8 %collective-permute-done = bf16[2,128,4,128]{3,1,2,0:T(8,128)(2,1)S(1)} collective-permute-done((bf16[2,128,4,128]{3,1,2,0:T(8,128)(2,1)}, bf16[2,128,4,128]{3,1,2,0:T(8,128)(2,1)S(1)}, u32[]{:S(2)}, u32[]{:S(2)}) %collective-permute-start) | collective-permute-done | bytes 262176 | tf_op jit(solution)/shard_map/while/body/eval_jaxpr/ppermute | solution.py:13
  63.0 3.3 conditional.8
  66.3 4.5 collective-permute-done
  73.6 3.3 conditional.8
  76.9 4.5 collective-permute-done
  84.2 3.3 conditional.8
  87.5 4.6 collective-permute-done
  94.9 3.3 conditional.8
  98.3 5.7 collective-permute-done
  106.7 3.3 conditional.8
  110.1 6.9 collective-permute-done
  119.8 3.3 conditional.8
  123.1 6.6 collective-permute-done
  132.4 3.3 conditional.8
  135.8 5.7 collective-permute-done
  144.3 3.3 conditional.8
  147.6 4.8 collective-permute-done
  155.3 3.3 conditional.8
  158.6 4.5 collective-permute-done
  165.9 3.3 conditional.8
  169.2 4.5 collective-permute-done
  176.5 3.3 conditional.8
  179.8 5.2 collective-permute-done
  192.8 315.9 %while.43 = (s32[]{:T(128)}, f32[128,4,4,128]{3,0,2,1:T(8,128)}, bf16[2,128,4,128]{3,1,2,0:T(8,128)(2,1)S(1)}, f32[2,128,4,128]{3,1,2,0:T(8,128)S(1)}, s32[]{:T(...) while((s32[]{:T(128)}, f32[128,4,4,128]{3,0,2,1:T(8,128)}, ...), condition=%wide.region_18.19_spmd.clone, body=%wide.region_14.0_spmd.clone.sunk | while | flops 338576288 | bytes 17750600 | solution.py:215
  196.0 5.3 conditional.9
  203.3 10.5 %collective-permute-done.2 = bf16[2,128,4,128]{3,1,2,0:T(8,128)(2,1)S(1)} collective-permute-done((bf16[2,128,4,128]{3,1,2,0:T(8,128)(2,1)}, bf16[2,128,4,128]{3,1,2,0:T(8,128)(2,1)S(1)}, u32[]{:S(2)}, u32[]{:S(2)}) %collective-permute-start.2) | collective-permute-done | bytes 262176 | tf_op jit(solution)/shard_map/while/body/eval_jaxpr/ppermute | solution.py:13
  217.0 5.3 conditional.9
  223.1 2.4 select_add_fusion.3
  225.5 10.2 %collective-permute-done.2 = bf16[2,128,4,128]{3,1,2,0:T(8,128)(2,1)S(1)} collective-permute-done((bf16[2,128,4,128]{3,1,2,0:T(8,128)(2,1)}, bf16[2,128,4,128]{3,1,2,0:T(8,128)(2,1)S(1)}, u32[]{:S(2)}, u32[]{:S(2)}) %collective-permute-start.2) | collective-permute-done | bytes 262176 | tf_op jit(solution)/shard_map/while/body/eval_jaxpr/ppermute | solution.py:13
  239.0 5.3 conditional.9
  247.5 9.4 %collective-permute-done.2 = bf16[2,128,4,128]{3,1,2,0:T(8,128)(2,1)S(1)} collective-permute-done((bf16[2,128,4,128]{3,1,2,0:T(8,128)(2,1)}, bf16[2,128,4,128]{3,1,2,0:T(8,128)(2,1)S(1)}, u32[]{:S(2)}, u32[]{:S(2)}) %collective-permute-start.2) | collective-permute-done | bytes 262176 | tf_op jit(solution)/shard_map/while/body/eval_jaxpr/ppermute | solution.py:13
  263.5 13.6 %collective-permute-done.2 = bf16[2,128,4,128]{3,1,2,0:T(8,128)(2,1)S(1)} collective-permute-done((bf16[2,128,4,128]{3,1,2,0:T(8,128)(2,1)}, bf16[2,128,4,128]{3,1,2,0:T(8,128)(2,1)S(1)}, u32[]{:S(2)}, u32[]{:S(2)}) %collective-permute-start.2) | collective-permute-done | bytes 262176 | tf_op jit(solution)/shard_map/while/body/eval_jaxpr/ppermute | solution.py:13
  280.5 5.3 conditional.9
  288.9 7.6 %collective-permute-done.2 = bf16[2,128,4,128]{3,1,2,0:T(8,128)(2,1)S(1)} collective-permute-done((bf16[2,128,4,128]{3,1,2,0:T(8,128)(2,1)}, bf16[2,128,4,128]{3,1,2,0:T(8,128)(2,1)S(1)}, u32[]{:S(2)}, u32[]{:S(2)}) %collective-permute-start.2) | collective-permute-done | bytes 262176 | tf_op jit(solution)/shard_map/while/body/eval_jaxpr/ppermute | solution.py:13
  299.9 5.3 conditional.9
  308.3 7.5 %collective-permute-done.2 = bf16[2,128,4,128]{3,1,2,0:T(8,128)(2,1)S(1)} collective-permute-done((bf16[2,128,4,128]{3,1,2,0:T(8,128)(2,1)}, bf16[2,128,4,128]{3,1,2,0:T(8,128)(2,1)S(1)}, u32[]{:S(2)}, u32[]{:S(2)}) %collective-permute-start.2) | collective-permute-done | bytes 262176 | tf_op jit(solution)/shard_map/while/body/eval_jaxpr/ppermute | solution.py:13
  319.1 5.3 conditional.9
  327.6 7.5 %collective-permute-done.2 = bf16[2,128,4,128]{3,1,2,0:T(8,128)(2,1)S(1)} collective-permute-done((bf16[2,128,4,128]{3,1,2,0:T(8,128)(2,1)}, bf16[2,128,4,128]{3,1,2,0:T(8,128)(2,1)S(1)}, u32[]{:S(2)}, u32[]{:S(2)}) %collective-permute-start.2) | collective-permute-done | bytes 262176 | tf_op jit(solution)/shard_map/while/body/eval_jaxpr/ppermute | solution.py:13
  338.4 5.3 conditional.9
  346.9 7.5 %collective-permute-done.2 = bf16[2,128,4,128]{3,1,2,0:T(8,128)(2,1)S(1)} collective-permute-done((bf16[2,128,4,128]{3,1,2,0:T(8,128)(2,1)}, bf16[2,128,4,128]{3,1,2,0:T(8,128)(2,1)S(1)}, u32[]{:S(2)}, u32[]{:S(2)}) %collective-permute-start.2) | collective-permute-done | bytes 262176 | tf_op jit(solution)/shard_map/while/body/eval_jaxpr/ppermute | solution.py:13
  357.7 5.3 conditional.9
  366.1 7.5 %collective-permute-done.2 = bf16[2,128,4,128]{3,1,2,0:T(8,128)(2,1)S(1)} collective-permute-done((bf16[2,128,4,128]{3,1,2,0:T(8,128)(2,1)}, bf16[2,128,4,128]{3,1,2,0:T(8,128)(2,1)S(1)}, u32[]{:S(2)}, u32[]{:S(2)}) %collective-permute-start.2) | collective-permute-done | bytes 262176 | tf_op jit(solution)/shard_map/while/body/eval_jaxpr/ppermute | solution.py:13
  377.0 5.3 conditional.9
  385.4 7.5 %collective-permute-done.2 = bf16[2,128,4,128]{3,1,2,0:T(8,128)(2,1)S(1)} collective-permute-done((bf16[2,128,4,128]{3,1,2,0:T(8,128)(2,1)}, bf16[2,128,4,128]{3,1,2,0:T(8,128)(2,1)S(1)}, u32[]{:S(2)}, u32[]{:S(2)}) %collective-permute-start.2) | collective-permute-done | bytes 262176 | tf_op jit(solution)/shard_map/while/body/eval_jaxpr/ppermute | solution.py:13
  396.2 5.3 conditional.9
  404.7 7.5 %collective-permute-done.2 = bf16[2,128,4,128]{3,1,2,0:T(8,128)(2,1)S(1)} collective-permute-done((bf16[2,128,4,128]{3,1,2,0:T(8,128)(2,1)}, bf16[2,128,4,128]{3,1,2,0:T(8,128)(2,1)S(1)}, u32[]{:S(2)}, u32[]{:S(2)}) %collective-permute-start.2) | collective-permute-done | bytes 262176 | tf_op jit(solution)/shard_map/while/body/eval_jaxpr/ppermute | solution.py:13
  415.5 5.3 conditional.9
  424.0 7.5 %collective-permute-done.2 = bf16[2,128,4,128]{3,1,2,0:T(8,128)(2,1)S(1)} collective-permute-done((bf16[2,128,4,128]{3,1,2,0:T(8,128)(2,1)}, bf16[2,128,4,128]{3,1,2,0:T(8,128)(2,1)S(1)}, u32[]{:S(2)}, u32[]{:S(2)}) %collective-permute-start.2) | collective-permute-done | bytes 262176 | tf_op jit(solution)/shard_map/while/body/eval_jaxpr/ppermute | solution.py:13
  434.8 5.3 conditional.9
  443.2 7.5 %collective-permute-done.2 = bf16[2,128,4,128]{3,1,2,0:T(8,128)(2,1)S(1)} collective-permute-done((bf16[2,128,4,128]{3,1,2,0:T(8,128)(2,1)}, bf16[2,128,4,128]{3,1,2,0:T(8,128)(2,1)S(1)}, u32[]{:S(2)}, u32[]{:S(2)}) %collective-permute-start.2) | collective-permute-done | bytes 262176 | tf_op jit(solution)/shard_map/while/body/eval_jaxpr/ppermute | solution.py:13
  454.1 5.3 conditional.9
  462.5 7.5 %collective-permute-done.2 = bf16[2,128,4,128]{3,1,2,0:T(8,128)(2,1)S(1)} collective-permute-done((bf16[2,128,4,128]{3,1,2,0:T(8,128)(2,1)}, bf16[2,128,4,128]{3,1,2,0:T(8,128)(2,1)S(1)}, u32[]{:S(2)}, u32[]{:S(2)}) %collective-permute-start.2) | collective-permute-done | bytes 262176 | tf_op jit(solution)/shard_map/while/body/eval_jaxpr/ppermute | solution.py:13
  473.3 5.3 conditional.9
  481.8 7.5 %collective-permute-done.2 = bf16[2,128,4,128]{3,1,2,0:T(8,128)(2,1)S(1)} collective-permute-done((bf16[2,128,4,128]{3,1,2,0:T(8,128)(2,1)}, bf16[2,128,4,128]{3,1,2,0:T(8,128)(2,1)S(1)}, u32[]{:S(2)}, u32[]{:S(2)}) %collective-permute-start.2) | collective-permute-done | bytes 262176 | tf_op jit(solution)/shard_map/while/body/eval_jaxpr/ppermute | solution.py:13
  492.6 5.3 conditional.9
  501.1 7.5 %collective-permute-done.2 = bf16[2,128,4,128]{3,1,2,0:T(8,128)(2,1)S(1)} collective-permute-done((bf16[2,128,4,128]{3,1,2,0:T(8,128)(2,1)}, bf16[2,128,4,128]{3,1,2,0:T(8,128)(2,1)S(1)}, u32[]{:S(2)}, u32[]{:S(2)}) %collective-permute-start.2) | collective-permute-done | bytes 262176 | tf_op jit(solution)/shard_map/while/body/eval_jaxpr/ppermute | solution.py:13
  514.5 174.3 %psum.7 = f32[16]{0:T(128)S(1)} all-reduce(f32[16]{0:T(128)S(1)} %convolution_bitcast_fusion.6), channel_id=1, replica_groups=mesh['pipe'=2,'ctx'=16,'dp'=4] {'ctx','dp'}, use_global_device_ids=true, to_apply=%region_22.23 | all-reduce | flops 16 | bytes 128 | tf_op jit(solution)/shard_map/psum | solution.py:228
  (668 shorter events, 263.9 us)
Async XLA Ops:
  0.6 3.7 copy-start
  0.6 10.1 %collective-permute-start.3 = (bf16[1,1,128,2048]{3,2,1,0:T(8,128)(2,1)}, bf16[1,1,128,2048]{3,2,1,0:T(8,128)(2,1)S(1)}, u32[]{:S(2)}, u32[]{:S(2)}) collective-permute-start(bf16[1,1,128,2048]{3,2,1,0:T(8,128)(2,1)} %param.21), channel_id=1, source_target_pairs={{0,64},{64,0},{1,65},{65,1},{2,66},{66,2},{3,67},{67,3},{4,68},{68... | collective-permute-start | bytes 1572872 | tf_op jit(solution)/shard_map/ppermute | solution.py:13
  0.7 3.5 copy-start.18
  2.8 186.4 %collective-permute-start.4 = (bf16[1,1,128,2048]{2,3,1,0:T(8,128)(2,1)}, bf16[1,1,128,2048]{2,3,1,0:T(8,128)(2,1)}, u32[]{:S(2)}, u32[]{:S(2)}) collective-permute-start(bf16[1,1,128,2048]{2,3,1,0:T(8,128)(2,1)} %copy.95), channel_id=1, source_target_pairs={{0,64},{64,0},{1,65},{65,1},{2,66},{66,2},{3,67},{67,3},{4,68},{68... | collective-permute-start | bytes 1572872 | tf_op jit(solution)/shard_map/ppermute | solution.py:13
  6.2 4.9 copy-start.13
  6.8 4.0 copy-start.17
  11.6 1.0 copy-start.8
  13.0 1.0 copy-start.4
  14.7 12.0 %collective-permute-start = (bf16[2,128,4,128]{3,1,2,0:T(8,128)(2,1)}, bf16[2,128,4,128]{3,1,2,0:T(8,128)(2,1)S(1)}, u32[]{:S(2)}, u32[]{:S(2)}) collective-permute-start(bf16[2,128,4,128]{3,1,2,0:T(8,128)(2,1)} %copy.144), channel_id=1, source_target_pairs={{0,4},{4,8},{8,12},{12,16},{16,20},{20,24},{24,28},{28,32},{32,36}... | collective-permute-start | bytes 786440 | tf_op jit(solution)/shard_map/while/body/eval_jaxpr/ppermute | solution.py:13
  27.4 11.2 %collective-permute-start = (bf16[2,128,4,128]{3,1,2,0:T(8,128)(2,1)}, bf16[2,128,4,128]{3,1,2,0:T(8,128)(2,1)S(1)}, u32[]{:S(2)}, u32[]{:S(2)}) collective-permute-start(bf16[2,128,4,128]{3,1,2,0:T(8,128)(2,1)} %copy.144), channel_id=1, source_target_pairs={{0,4},{4,8},{8,12},{12,16},{16,20},{20,24},{24,28},{28,32},{32,36}... | collective-permute-start | bytes 786440 | tf_op jit(solution)/shard_map/while/body/eval_jaxpr/ppermute | solution.py:13
  39.3 10.3 %collective-permute-start = (bf16[2,128,4,128]{3,1,2,0:T(8,128)(2,1)}, bf16[2,128,4,128]{3,1,2,0:T(8,128)(2,1)S(1)}, u32[]{:S(2)}, u32[]{:S(2)}) collective-permute-start(bf16[2,128,4,128]{3,1,2,0:T(8,128)(2,1)} %copy.144), channel_id=1, source_target_pairs={{0,4},{4,8},{8,12},{12,16},{16,20},{20,24},{24,28},{28,32},{32,36}... | collective-permute-start | bytes 786440 | tf_op jit(solution)/shard_map/while/body/eval_jaxpr/ppermute | solution.py:13
  50.3 9.9 %collective-permute-start = (bf16[2,128,4,128]{3,1,2,0:T(8,128)(2,1)}, bf16[2,128,4,128]{3,1,2,0:T(8,128)(2,1)S(1)}, u32[]{:S(2)}, u32[]{:S(2)}) collective-permute-start(bf16[2,128,4,128]{3,1,2,0:T(8,128)(2,1)} %copy.144), channel_id=1, source_target_pairs={{0,4},{4,8},{8,12},{12,16},{16,20},{20,24},{24,28},{28,32},{32,36}... | collective-permute-start | bytes 786440 | tf_op jit(solution)/shard_map/while/body/eval_jaxpr/ppermute | solution.py:13
  60.9 9.9 %collective-permute-start = (bf16[2,128,4,128]{3,1,2,0:T(8,128)(2,1)}, bf16[2,128,4,128]{3,1,2,0:T(8,128)(2,1)S(1)}, u32[]{:S(2)}, u32[]{:S(2)}) collective-permute-start(bf16[2,128,4,128]{3,1,2,0:T(8,128)(2,1)} %copy.144), channel_id=1, source_target_pairs={{0,4},{4,8},{8,12},{12,16},{16,20},{20,24},{24,28},{28,32},{32,36}... | collective-permute-start | bytes 786440 | tf_op jit(solution)/shard_map/while/body/eval_jaxpr/ppermute | solution.py:13
  71.5 9.9 %collective-permute-start = (bf16[2,128,4,128]{3,1,2,0:T(8,128)(2,1)}, bf16[2,128,4,128]{3,1,2,0:T(8,128)(2,1)S(1)}, u32[]{:S(2)}, u32[]{:S(2)}) collective-permute-start(bf16[2,128,4,128]{3,1,2,0:T(8,128)(2,1)} %copy.144), channel_id=1, source_target_pairs={{0,4},{4,8},{8,12},{12,16},{16,20},{20,24},{24,28},{28,32},{32,36}... | collective-permute-start | bytes 786440 | tf_op jit(solution)/shard_map/while/body/eval_jaxpr/ppermute | solution.py:13
  82.1 10.0 %collective-permute-start = (bf16[2,128,4,128]{3,1,2,0:T(8,128)(2,1)}, bf16[2,128,4,128]{3,1,2,0:T(8,128)(2,1)S(1)}, u32[]{:S(2)}, u32[]{:S(2)}) collective-permute-start(bf16[2,128,4,128]{3,1,2,0:T(8,128)(2,1)} %copy.144), channel_id=1, source_target_pairs={{0,4},{4,8},{8,12},{12,16},{16,20},{20,24},{24,28},{28,32},{32,36}... | collective-permute-start | bytes 786440 | tf_op jit(solution)/shard_map/while/body/eval_jaxpr/ppermute | solution.py:13
  92.9 11.1 %collective-permute-start = (bf16[2,128,4,128]{3,1,2,0:T(8,128)(2,1)}, bf16[2,128,4,128]{3,1,2,0:T(8,128)(2,1)S(1)}, u32[]{:S(2)}, u32[]{:S(2)}) collective-permute-start(bf16[2,128,4,128]{3,1,2,0:T(8,128)(2,1)} %copy.144), channel_id=1, source_target_pairs={{0,4},{4,8},{8,12},{12,16},{16,20},{20,24},{24,28},{28,32},{32,36}... | collective-permute-start | bytes 786440 | tf_op jit(solution)/shard_map/while/body/eval_jaxpr/ppermute | solution.py:13
  104.7 12.3 %collective-permute-start = (bf16[2,128,4,128]{3,1,2,0:T(8,128)(2,1)}, bf16[2,128,4,128]{3,1,2,0:T(8,128)(2,1)S(1)}, u32[]{:S(2)}, u32[]{:S(2)}) collective-permute-start(bf16[2,128,4,128]{3,1,2,0:T(8,128)(2,1)} %copy.144), channel_id=1, source_target_pairs={{0,4},{4,8},{8,12},{12,16},{16,20},{20,24},{24,28},{28,32},{32,36}... | collective-permute-start | bytes 786440 | tf_op jit(solution)/shard_map/while/body/eval_jaxpr/ppermute | solution.py:13
  117.7 12.0 %collective-permute-start = (bf16[2,128,4,128]{3,1,2,0:T(8,128)(2,1)}, bf16[2,128,4,128]{3,1,2,0:T(8,128)(2,1)S(1)}, u32[]{:S(2)}, u32[]{:S(2)}) collective-permute-start(bf16[2,128,4,128]{3,1,2,0:T(8,128)(2,1)} %copy.144), channel_id=1, source_target_pairs={{0,4},{4,8},{8,12},{12,16},{16,20},{20,24},{24,28},{28,32},{32,36}... | collective-permute-start | bytes 786440 | tf_op jit(solution)/shard_map/while/body/eval_jaxpr/ppermute | solution.py:13
  130.4 11.1 %collective-permute-start = (bf16[2,128,4,128]{3,1,2,0:T(8,128)(2,1)}, bf16[2,128,4,128]{3,1,2,0:T(8,128)(2,1)S(1)}, u32[]{:S(2)}, u32[]{:S(2)}) collective-permute-start(bf16[2,128,4,128]{3,1,2,0:T(8,128)(2,1)} %copy.144), channel_id=1, source_target_pairs={{0,4},{4,8},{8,12},{12,16},{16,20},{20,24},{24,28},{28,32},{32,36}... | collective-permute-start | bytes 786440 | tf_op jit(solution)/shard_map/while/body/eval_jaxpr/ppermute | solution.py:13
  142.2 10.2 %collective-permute-start = (bf16[2,128,4,128]{3,1,2,0:T(8,128)(2,1)}, bf16[2,128,4,128]{3,1,2,0:T(8,128)(2,1)S(1)}, u32[]{:S(2)}, u32[]{:S(2)}) collective-permute-start(bf16[2,128,4,128]{3,1,2,0:T(8,128)(2,1)} %copy.144), channel_id=1, source_target_pairs={{0,4},{4,8},{8,12},{12,16},{16,20},{20,24},{24,28},{28,32},{32,36}... | collective-permute-start | bytes 786440 | tf_op jit(solution)/shard_map/while/body/eval_jaxpr/ppermute | solution.py:13
  153.2 9.9 %collective-permute-start = (bf16[2,128,4,128]{3,1,2,0:T(8,128)(2,1)}, bf16[2,128,4,128]{3,1,2,0:T(8,128)(2,1)S(1)}, u32[]{:S(2)}, u32[]{:S(2)}) collective-permute-start(bf16[2,128,4,128]{3,1,2,0:T(8,128)(2,1)} %copy.144), channel_id=1, source_target_pairs={{0,4},{4,8},{8,12},{12,16},{16,20},{20,24},{24,28},{28,32},{32,36}... | collective-permute-start | bytes 786440 | tf_op jit(solution)/shard_map/while/body/eval_jaxpr/ppermute | solution.py:13
  163.8 9.9 %collective-permute-start = (bf16[2,128,4,128]{3,1,2,0:T(8,128)(2,1)}, bf16[2,128,4,128]{3,1,2,0:T(8,128)(2,1)S(1)}, u32[]{:S(2)}, u32[]{:S(2)}) collective-permute-start(bf16[2,128,4,128]{3,1,2,0:T(8,128)(2,1)} %copy.144), channel_id=1, source_target_pairs={{0,4},{4,8},{8,12},{12,16},{16,20},{20,24},{24,28},{28,32},{32,36}... | collective-permute-start | bytes 786440 | tf_op jit(solution)/shard_map/while/body/eval_jaxpr/ppermute | solution.py:13
  174.4 10.6 %collective-permute-start = (bf16[2,128,4,128]{3,1,2,0:T(8,128)(2,1)}, bf16[2,128,4,128]{3,1,2,0:T(8,128)(2,1)S(1)}, u32[]{:S(2)}, u32[]{:S(2)}) collective-permute-start(bf16[2,128,4,128]{3,1,2,0:T(8,128)(2,1)} %copy.144), channel_id=1, source_target_pairs={{0,4},{4,8},{8,12},{12,16},{16,20},{20,24},{24,28},{28,32},{32,36}... | collective-permute-start | bytes 786440 | tf_op jit(solution)/shard_map/while/body/eval_jaxpr/ppermute | solution.py:13
  186.7 1.3 copy-start.7
  186.7 1.3 copy-start.9
  189.3 1.4 copy-start.10
  190.7 2.1 copy-start.3
  193.5 20.3 %collective-permute-start.1 = (bf16[2,128,4,128]{3,1,2,0:T(8,128)(2,1)}, bf16[2,128,4,128]{3,1,2,0:T(8,128)(2,1)S(1)}, u32[]{:S(2)}, u32[]{:S(2)}) collective-permute-start(bf16[2,128,4,128]{3,1,2,0:T(8,128)(2,1)} %copy.162), channel_id=1, source_target_pairs={{0,4},{4,8},{8,12},{12,16},{16,20},{20,24},{24,28},{28,32},{32,36}... | collective-permute-start | bytes 786440 | tf_op jit(solution)/shard_map/while/body/eval_jaxpr/ppermute | solution.py:13
  202.1 11.6 %collective-permute-start.2 = (bf16[2,128,4,128]{3,1,2,0:T(8,128)(2,1)}, bf16[2,128,4,128]{3,1,2,0:T(8,128)(2,1)S(1)}, u32[]{:S(2)}, u32[]{:S(2)}) collective-permute-start(bf16[2,128,4,128]{3,1,2,0:T(8,128)(2,1)} %fusion.77), channel_id=1, source_target_pairs={{0,4},{4,8},{8,12},{12,16},{16,20},{20,24},{24,28},{28,32},{32,36}... | collective-permute-start | bytes 786440 | tf_op jit(solution)/shard_map/while/body/eval_jaxpr/ppermute | solution.py:13
  214.5 21.3 %collective-permute-start.1 = (bf16[2,128,4,128]{3,1,2,0:T(8,128)(2,1)}, bf16[2,128,4,128]{3,1,2,0:T(8,128)(2,1)S(1)}, u32[]{:S(2)}, u32[]{:S(2)}) collective-permute-start(bf16[2,128,4,128]{3,1,2,0:T(8,128)(2,1)} %copy.162), channel_id=1, source_target_pairs={{0,4},{4,8},{8,12},{12,16},{16,20},{20,24},{24,28},{28,32},{32,36}... | collective-permute-start | bytes 786440 | tf_op jit(solution)/shard_map/while/body/eval_jaxpr/ppermute | solution.py:13
  223.1 12.6 %collective-permute-start.2 = (bf16[2,128,4,128]{3,1,2,0:T(8,128)(2,1)}, bf16[2,128,4,128]{3,1,2,0:T(8,128)(2,1)S(1)}, u32[]{:S(2)}, u32[]{:S(2)}) collective-permute-start(bf16[2,128,4,128]{3,1,2,0:T(8,128)(2,1)} %fusion.77), channel_id=1, source_target_pairs={{0,4},{4,8},{8,12},{12,16},{16,20},{20,24},{24,28},{28,32},{32,36}... | collective-permute-start | bytes 786440 | tf_op jit(solution)/shard_map/while/body/eval_jaxpr/ppermute | solution.py:13
  236.5 20.4 %collective-permute-start.1 = (bf16[2,128,4,128]{3,1,2,0:T(8,128)(2,1)}, bf16[2,128,4,128]{3,1,2,0:T(8,128)(2,1)S(1)}, u32[]{:S(2)}, u32[]{:S(2)}) collective-permute-start(bf16[2,128,4,128]{3,1,2,0:T(8,128)(2,1)} %copy.162), channel_id=1, source_target_pairs={{0,4},{4,8},{8,12},{12,16},{16,20},{20,24},{24,28},{28,32},{32,36}... | collective-permute-start | bytes 786440 | tf_op jit(solution)/shard_map/while/body/eval_jaxpr/ppermute | solution.py:13
  245.1 11.8 %collective-permute-start.2 = (bf16[2,128,4,128]{3,1,2,0:T(8,128)(2,1)}, bf16[2,128,4,128]{3,1,2,0:T(8,128)(2,1)S(1)}, u32[]{:S(2)}, u32[]{:S(2)}) collective-permute-start(bf16[2,128,4,128]{3,1,2,0:T(8,128)(2,1)} %fusion.77), channel_id=1, source_target_pairs={{0,4},{4,8},{8,12},{12,16},{16,20},{20,24},{24,28},{28,32},{32,36}... | collective-permute-start | bytes 786440 | tf_op jit(solution)/shard_map/while/body/eval_jaxpr/ppermute | solution.py:13
  257.6 19.6 %collective-permute-start.1 = (bf16[2,128,4,128]{3,1,2,0:T(8,128)(2,1)}, bf16[2,128,4,128]{3,1,2,0:T(8,128)(2,1)S(1)}, u32[]{:S(2)}, u32[]{:S(2)}) collective-permute-start(bf16[2,128,4,128]{3,1,2,0:T(8,128)(2,1)} %copy.162), channel_id=1, source_target_pairs={{0,4},{4,8},{8,12},{12,16},{16,20},{20,24},{24,28},{28,32},{32,36}... | collective-permute-start | bytes 786440 | tf_op jit(solution)/shard_map/while/body/eval_jaxpr/ppermute | solution.py:13
  261.1 16.0 %collective-permute-start.2 = (bf16[2,128,4,128]{3,1,2,0:T(8,128)(2,1)}, bf16[2,128,4,128]{3,1,2,0:T(8,128)(2,1)S(1)}, u32[]{:S(2)}, u32[]{:S(2)}) collective-permute-start(bf16[2,128,4,128]{3,1,2,0:T(8,128)(2,1)} %fusion.77), channel_id=1, source_target_pairs={{0,4},{4,8},{8,12},{12,16},{16,20},{20,24},{24,28},{28,32},{32,36}... | collective-permute-start | bytes 786440 | tf_op jit(solution)/shard_map/while/body/eval_jaxpr/ppermute | solution.py:13
  277.9 18.6 %collective-permute-start.1 = (bf16[2,128,4,128]{3,1,2,0:T(8,128)(2,1)}, bf16[2,128,4,128]{3,1,2,0:T(8,128)(2,1)S(1)}, u32[]{:S(2)}, u32[]{:S(2)}) collective-permute-start(bf16[2,128,4,128]{3,1,2,0:T(8,128)(2,1)} %copy.162), channel_id=1, source_target_pairs={{0,4},{4,8},{8,12},{12,16},{16,20},{20,24},{24,28},{28,32},{32,36}... | collective-permute-start | bytes 786440 | tf_op jit(solution)/shard_map/while/body/eval_jaxpr/ppermute | solution.py:13
  286.5 10.0 %collective-permute-start.2 = (bf16[2,128,4,128]{3,1,2,0:T(8,128)(2,1)}, bf16[2,128,4,128]{3,1,2,0:T(8,128)(2,1)S(1)}, u32[]{:S(2)}, u32[]{:S(2)}) collective-permute-start(bf16[2,128,4,128]{3,1,2,0:T(8,128)(2,1)} %fusion.77), channel_id=1, source_target_pairs={{0,4},{4,8},{8,12},{12,16},{16,20},{20,24},{24,28},{28,32},{32,36}... | collective-permute-start | bytes 786440 | tf_op jit(solution)/shard_map/while/body/eval_jaxpr/ppermute | solution.py:13
  297.3 18.5 %collective-permute-start.1 = (bf16[2,128,4,128]{3,1,2,0:T(8,128)(2,1)}, bf16[2,128,4,128]{3,1,2,0:T(8,128)(2,1)S(1)}, u32[]{:S(2)}, u32[]{:S(2)}) collective-permute-start(bf16[2,128,4,128]{3,1,2,0:T(8,128)(2,1)} %copy.162), channel_id=1, source_target_pairs={{0,4},{4,8},{8,12},{12,16},{16,20},{20,24},{24,28},{28,32},{32,36}... | collective-permute-start | bytes 786440 | tf_op jit(solution)/shard_map/while/body/eval_jaxpr/ppermute | solution.py:13
  305.9 9.9 %collective-permute-start.2 = (bf16[2,128,4,128]{3,1,2,0:T(8,128)(2,1)}, bf16[2,128,4,128]{3,1,2,0:T(8,128)(2,1)S(1)}, u32[]{:S(2)}, u32[]{:S(2)}) collective-permute-start(bf16[2,128,4,128]{3,1,2,0:T(8,128)(2,1)} %fusion.77), channel_id=1, source_target_pairs={{0,4},{4,8},{8,12},{12,16},{16,20},{20,24},{24,28},{28,32},{32,36}... | collective-permute-start | bytes 786440 | tf_op jit(solution)/shard_map/while/body/eval_jaxpr/ppermute | solution.py:13
  316.6 18.5 %collective-permute-start.1 = (bf16[2,128,4,128]{3,1,2,0:T(8,128)(2,1)}, bf16[2,128,4,128]{3,1,2,0:T(8,128)(2,1)S(1)}, u32[]{:S(2)}, u32[]{:S(2)}) collective-permute-start(bf16[2,128,4,128]{3,1,2,0:T(8,128)(2,1)} %copy.162), channel_id=1, source_target_pairs={{0,4},{4,8},{8,12},{12,16},{16,20},{20,24},{24,28},{28,32},{32,36}... | collective-permute-start | bytes 786440 | tf_op jit(solution)/shard_map/while/body/eval_jaxpr/ppermute | solution.py:13
  325.2 9.9 %collective-permute-start.2 = (bf16[2,128,4,128]{3,1,2,0:T(8,128)(2,1)}, bf16[2,128,4,128]{3,1,2,0:T(8,128)(2,1)S(1)}, u32[]{:S(2)}, u32[]{:S(2)}) collective-permute-start(bf16[2,128,4,128]{3,1,2,0:T(8,128)(2,1)} %fusion.77), channel_id=1, source_target_pairs={{0,4},{4,8},{8,12},{12,16},{16,20},{20,24},{24,28},{28,32},{32,36}... | collective-permute-start | bytes 786440 | tf_op jit(solution)/shard_map/while/body/eval_jaxpr/ppermute | solution.py:13
  335.9 18.5 %collective-permute-start.1 = (bf16[2,128,4,128]{3,1,2,0:T(8,128)(2,1)}, bf16[2,128,4,128]{3,1,2,0:T(8,128)(2,1)S(1)}, u32[]{:S(2)}, u32[]{:S(2)}) collective-permute-start(bf16[2,128,4,128]{3,1,2,0:T(8,128)(2,1)} %copy.162), channel_id=1, source_target_pairs={{0,4},{4,8},{8,12},{12,16},{16,20},{20,24},{24,28},{28,32},{32,36}... | collective-permute-start | bytes 786440 | tf_op jit(solution)/shard_map/while/body/eval_jaxpr/ppermute | solution.py:13
  344.5 9.9 %collective-permute-start.2 = (bf16[2,128,4,128]{3,1,2,0:T(8,128)(2,1)}, bf16[2,128,4,128]{3,1,2,0:T(8,128)(2,1)S(1)}, u32[]{:S(2)}, u32[]{:S(2)}) collective-permute-start(bf16[2,128,4,128]{3,1,2,0:T(8,128)(2,1)} %fusion.77), channel_id=1, source_target_pairs={{0,4},{4,8},{8,12},{12,16},{16,20},{20,24},{24,28},{28,32},{32,36}... | collective-permute-start | bytes 786440 | tf_op jit(solution)/shard_map/while/body/eval_jaxpr/ppermute | solution.py:13
  355.1 18.5 %collective-permute-start.1 = (bf16[2,128,4,128]{3,1,2,0:T(8,128)(2,1)}, bf16[2,128,4,128]{3,1,2,0:T(8,128)(2,1)S(1)}, u32[]{:S(2)}, u32[]{:S(2)}) collective-permute-start(bf16[2,128,4,128]{3,1,2,0:T(8,128)(2,1)} %copy.162), channel_id=1, source_target_pairs={{0,4},{4,8},{8,12},{12,16},{16,20},{20,24},{24,28},{28,32},{32,36}... | collective-permute-start | bytes 786440 | tf_op jit(solution)/shard_map/while/body/eval_jaxpr/ppermute | solution.py:13
  363.7 9.9 %collective-permute-start.2 = (bf16[2,128,4,128]{3,1,2,0:T(8,128)(2,1)}, bf16[2,128,4,128]{3,1,2,0:T(8,128)(2,1)S(1)}, u32[]{:S(2)}, u32[]{:S(2)}) collective-permute-start(bf16[2,128,4,128]{3,1,2,0:T(8,128)(2,1)} %fusion.77), channel_id=1, source_target_pairs={{0,4},{4,8},{8,12},{12,16},{16,20},{20,24},{24,28},{28,32},{32,36}... | collective-permute-start | bytes 786440 | tf_op jit(solution)/shard_map/while/body/eval_jaxpr/ppermute | solution.py:13
  374.4 18.5 %collective-permute-start.1 = (bf16[2,128,4,128]{3,1,2,0:T(8,128)(2,1)}, bf16[2,128,4,128]{3,1,2,0:T(8,128)(2,1)S(1)}, u32[]{:S(2)}, u32[]{:S(2)}) collective-permute-start(bf16[2,128,4,128]{3,1,2,0:T(8,128)(2,1)} %copy.162), channel_id=1, source_target_pairs={{0,4},{4,8},{8,12},{12,16},{16,20},{20,24},{24,28},{28,32},{32,36}... | collective-permute-start | bytes 786440 | tf_op jit(solution)/shard_map/while/body/eval_jaxpr/ppermute | solution.py:13
  383.0 9.9 %collective-permute-start.2 = (bf16[2,128,4,128]{3,1,2,0:T(8,128)(2,1)}, bf16[2,128,4,128]{3,1,2,0:T(8,128)(2,1)S(1)}, u32[]{:S(2)}, u32[]{:S(2)}) collective-permute-start(bf16[2,128,4,128]{3,1,2,0:T(8,128)(2,1)} %fusion.77), channel_id=1, source_target_pairs={{0,4},{4,8},{8,12},{12,16},{16,20},{20,24},{24,28},{28,32},{32,36}... | collective-permute-start | bytes 786440 | tf_op jit(solution)/shard_map/while/body/eval_jaxpr/ppermute | solution.py:13
  393.7 18.5 %collective-permute-start.1 = (bf16[2,128,4,128]{3,1,2,0:T(8,128)(2,1)}, bf16[2,128,4,128]{3,1,2,0:T(8,128)(2,1)S(1)}, u32[]{:S(2)}, u32[]{:S(2)}) collective-permute-start(bf16[2,128,4,128]{3,1,2,0:T(8,128)(2,1)} %copy.162), channel_id=1, source_target_pairs={{0,4},{4,8},{8,12},{12,16},{16,20},{20,24},{24,28},{28,32},{32,36}... | collective-permute-start | bytes 786440 | tf_op jit(solution)/shard_map/while/body/eval_jaxpr/ppermute | solution.py:13
  402.3 9.9 %collective-permute-start.2 = (bf16[2,128,4,128]{3,1,2,0:T(8,128)(2,1)}, bf16[2,128,4,128]{3,1,2,0:T(8,128)(2,1)S(1)}, u32[]{:S(2)}, u32[]{:S(2)}) collective-permute-start(bf16[2,128,4,128]{3,1,2,0:T(8,128)(2,1)} %fusion.77), channel_id=1, source_target_pairs={{0,4},{4,8},{8,12},{12,16},{16,20},{20,24},{24,28},{28,32},{32,36}... | collective-permute-start | bytes 786440 | tf_op jit(solution)/shard_map/while/body/eval_jaxpr/ppermute | solution.py:13
  413.0 18.5 %collective-permute-start.1 = (bf16[2,128,4,128]{3,1,2,0:T(8,128)(2,1)}, bf16[2,128,4,128]{3,1,2,0:T(8,128)(2,1)S(1)}, u32[]{:S(2)}, u32[]{:S(2)}) collective-permute-start(bf16[2,128,4,128]{3,1,2,0:T(8,128)(2,1)} %copy.162), channel_id=1, source_target_pairs={{0,4},{4,8},{8,12},{12,16},{16,20},{20,24},{24,28},{28,32},{32,36}... | collective-permute-start | bytes 786440 | tf_op jit(solution)/shard_map/while/body/eval_jaxpr/ppermute | solution.py:13
  421.6 9.9 %collective-permute-start.2 = (bf16[2,128,4,128]{3,1,2,0:T(8,128)(2,1)}, bf16[2,128,4,128]{3,1,2,0:T(8,128)(2,1)S(1)}, u32[]{:S(2)}, u32[]{:S(2)}) collective-permute-start(bf16[2,128,4,128]{3,1,2,0:T(8,128)(2,1)} %fusion.77), channel_id=1, source_target_pairs={{0,4},{4,8},{8,12},{12,16},{16,20},{20,24},{24,28},{28,32},{32,36}... | collective-permute-start | bytes 786440 | tf_op jit(solution)/shard_map/while/body/eval_jaxpr/ppermute | solution.py:13
  432.2 18.5 %collective-permute-start.1 = (bf16[2,128,4,128]{3,1,2,0:T(8,128)(2,1)}, bf16[2,128,4,128]{3,1,2,0:T(8,128)(2,1)S(1)}, u32[]{:S(2)}, u32[]{:S(2)}) collective-permute-start(bf16[2,128,4,128]{3,1,2,0:T(8,128)(2,1)} %copy.162), channel_id=1, source_target_pairs={{0,4},{4,8},{8,12},{12,16},{16,20},{20,24},{24,28},{28,32},{32,36}... | collective-permute-start | bytes 786440 | tf_op jit(solution)/shard_map/while/body/eval_jaxpr/ppermute | solution.py:13
  440.8 9.9 %collective-permute-start.2 = (bf16[2,128,4,128]{3,1,2,0:T(8,128)(2,1)}, bf16[2,128,4,128]{3,1,2,0:T(8,128)(2,1)S(1)}, u32[]{:S(2)}, u32[]{:S(2)}) collective-permute-start(bf16[2,128,4,128]{3,1,2,0:T(8,128)(2,1)} %fusion.77), channel_id=1, source_target_pairs={{0,4},{4,8},{8,12},{12,16},{16,20},{20,24},{24,28},{28,32},{32,36}... | collective-permute-start | bytes 786440 | tf_op jit(solution)/shard_map/while/body/eval_jaxpr/ppermute | solution.py:13
  451.5 18.5 %collective-permute-start.1 = (bf16[2,128,4,128]{3,1,2,0:T(8,128)(2,1)}, bf16[2,128,4,128]{3,1,2,0:T(8,128)(2,1)S(1)}, u32[]{:S(2)}, u32[]{:S(2)}) collective-permute-start(bf16[2,128,4,128]{3,1,2,0:T(8,128)(2,1)} %copy.162), channel_id=1, source_target_pairs={{0,4},{4,8},{8,12},{12,16},{16,20},{20,24},{24,28},{28,32},{32,36}... | collective-permute-start | bytes 786440 | tf_op jit(solution)/shard_map/while/body/eval_jaxpr/ppermute | solution.py:13
  460.1 9.9 %collective-permute-start.2 = (bf16[2,128,4,128]{3,1,2,0:T(8,128)(2,1)}, bf16[2,128,4,128]{3,1,2,0:T(8,128)(2,1)S(1)}, u32[]{:S(2)}, u32[]{:S(2)}) collective-permute-start(bf16[2,128,4,128]{3,1,2,0:T(8,128)(2,1)} %fusion.77), channel_id=1, source_target_pairs={{0,4},{4,8},{8,12},{12,16},{16,20},{20,24},{24,28},{28,32},{32,36}... | collective-permute-start | bytes 786440 | tf_op jit(solution)/shard_map/while/body/eval_jaxpr/ppermute | solution.py:13
  470.8 18.5 %collective-permute-start.1 = (bf16[2,128,4,128]{3,1,2,0:T(8,128)(2,1)}, bf16[2,128,4,128]{3,1,2,0:T(8,128)(2,1)S(1)}, u32[]{:S(2)}, u32[]{:S(2)}) collective-permute-start(bf16[2,128,4,128]{3,1,2,0:T(8,128)(2,1)} %copy.162), channel_id=1, source_target_pairs={{0,4},{4,8},{8,12},{12,16},{16,20},{20,24},{24,28},{28,32},{32,36}... | collective-permute-start | bytes 786440 | tf_op jit(solution)/shard_map/while/body/eval_jaxpr/ppermute | solution.py:13
  479.4 9.9 %collective-permute-start.2 = (bf16[2,128,4,128]{3,1,2,0:T(8,128)(2,1)}, bf16[2,128,4,128]{3,1,2,0:T(8,128)(2,1)S(1)}, u32[]{:S(2)}, u32[]{:S(2)}) collective-permute-start(bf16[2,128,4,128]{3,1,2,0:T(8,128)(2,1)} %fusion.77), channel_id=1, source_target_pairs={{0,4},{4,8},{8,12},{12,16},{16,20},{20,24},{24,28},{28,32},{32,36}... | collective-permute-start | bytes 786440 | tf_op jit(solution)/shard_map/while/body/eval_jaxpr/ppermute | solution.py:13
  490.1 18.5 %collective-permute-start.1 = (bf16[2,128,4,128]{3,1,2,0:T(8,128)(2,1)}, bf16[2,128,4,128]{3,1,2,0:T(8,128)(2,1)S(1)}, u32[]{:S(2)}, u32[]{:S(2)}) collective-permute-start(bf16[2,128,4,128]{3,1,2,0:T(8,128)(2,1)} %copy.162), channel_id=1, source_target_pairs={{0,4},{4,8},{8,12},{12,16},{16,20},{20,24},{24,28},{28,32},{32,36}... | collective-permute-start | bytes 786440 | tf_op jit(solution)/shard_map/while/body/eval_jaxpr/ppermute | solution.py:13
  498.7 9.9 %collective-permute-start.2 = (bf16[2,128,4,128]{3,1,2,0:T(8,128)(2,1)}, bf16[2,128,4,128]{3,1,2,0:T(8,128)(2,1)S(1)}, u32[]{:S(2)}, u32[]{:S(2)}) collective-permute-start(bf16[2,128,4,128]{3,1,2,0:T(8,128)(2,1)} %fusion.77), channel_id=1, source_target_pairs={{0,4},{4,8},{8,12},{12,16},{16,20},{20,24},{24,28},{28,32},{32,36}... | collective-permute-start | bytes 786440 | tf_op jit(solution)/shard_map/while/body/eval_jaxpr/ppermute | solution.py:13
  508.6 1.2 copy-start.1
  510.0 1.2 copy-start.5
  510.0 1.2 copy-start.14
  511.2 1.8 copy-start.12
  691.4 1.0 copy-start.11
  (23 other events, 15.3 us)
where the time goes:
time: 697 us; the launch traced here: 693 us
  waiting for transfers between devices  215 us (31%)
  blocking collectives  174 us (25%)
  matrix products  105 us (15%)
  other arithmetic  103 us (15%)
  local copies, waits for them, and re-layouts  54.2 us (8%)
  loops' own time  37.8 us (5%)
    ppermute x49, waiting for transfers between devices, passed_along(): lax.ppermute(value, axis, [(i, (i + by) % size) for i in range(size)])  215 us
    psum x1, blocking collectives, on_device(): summed_table = lax.psum(partial_value, ('ctx', 'dp'))  174 us
    add x16, other arithmetic, backward_turn(): query_sum = query_sum + query_part  37.1 us
    dot_general x15, matrix products, visit(): jnp.einsum('hgqk,khd->qhgd', weights.astype(jnp.bfloat16), block_pair[1],...  22.7 us
    while x31, local copies, waits for them, and re-layouts  22 us
    dot_general x15, matrix products, visit_back(): jnp.einsum('qhgd,khd->hgqk', grouped_queries, block_pair[0], preferred_el...  18.9 us
    dot_general x15, matrix products, visit_back(): jnp.einsum('hgqk,khd->qhgd', score_grad, block_pair[0], preferred_element...  18.9 us
    another operation x1, loops' own time, on_device(): lax.fori_loop(0, cycle_size, backward_turn, (empty_query, key_value, empt...  18.4 us
  transfers between devices with their start and end apart: 49, of which 31 were waited for; matrix products, arithmetic and copies ran while one was open for 32% of the time, Pallas kernels for 0%

commit v1 on v0

--- a/solution.py
+++ b/solution.py
@@ -225,7 +225,7 @@
     )
     log_gradient = -jnp.sum(angle_sums * angles, axis=0)
     partial_value = jnp.dot(log_gradient, onehot, precision=lax.Precision.HIGHEST)
-    summed_table = lax.psum(partial_value, ("ctx", "dp"))
+    summed_table = lax.psum(lax.psum(partial_value, "dp"), "ctx")
     table_grad = summed_table / (cycle_size * lax.axis_size("dp") * tok_rows)
     return (
         final_result.reshape(1, 1, tok_rows, q_width),

time: 697 us -> 573 us (0.82)
  blocking collectives: 174 us -> 47.1 us
    psum x1 -> x2, blocking collectives: 174 us -> 47.1 us  [on_device(): summed_table = lax.psum(lax.psum(partial_value, 'dp'), 'ctx')]
  transfers between devices with their start and end apart: 49 -> 49, of which waited for: 31 -> 31; matrix products, arithmetic and copies ran while one was open for 32% -> 39% of each run, Pallas kernels for 0% -> 0%
where the time goes in v1:
time: 573 us; the launch traced here: 569 us
  waiting for transfers between devices  213 us (37%)
  other arithmetic  105 us (18%)
  matrix products  105 us (18%)
  local copies, waits for them, and re-layouts  54.6 us (10%)
  blocking collectives  47.1 us (8%)
  loops' own time  40.9 us (7%)
    ppermute x49, waiting for transfers between devices, passed_along(): lax.ppermute(value, axis, [(i, (i + by) % size) for i in range(size)])  213 us
    psum x2, blocking collectives, on_device(): summed_table = lax.psum(lax.psum(partial_value, 'dp'), 'ctx')  47.1 us
    add x16, other arithmetic, backward_turn(): query_sum = query_sum + query_part  37 us
    dot_general x15, matrix products, visit(): jnp.einsum('hgqk,khd->qhgd', weights.astype(jnp.bfloat16), block_pair[1],...  22.7 us
    while x31, local copies, waits for them, and re-layouts  21.8 us
    another operation x1, loops' own time, on_device(): lax.fori_loop(0, cycle_size, backward_turn, (empty_query, key_value, empt...  19.9 us
    another operation x1, loops' own time, on_device(): lax.fori_loop(0, cycle_size - 1, forward_turn, (initial, key_value))  19.2 us
    dot_general x15, matrix products, visit_back(): jnp.einsum('qhgd,khd->hgqk', grouped_queries, block_pair[0], preferred_el...  18.9 us
  transfers between devices with their start and end apart: 49, of which 31 were waited for; matrix products, arithmetic and copies ran while one was open for 39% of the time, Pallas kernels for 0%

profile of v1, /device:TPU:0, one launch (start us, length us, event | category | flops | bytes accessed | tf_op | source)
XLA Modules:
  0.0 569.4 jit_solution(18210301716404365243)
XLA Ops:
  14.0 170.8 %while.42 = (s32[]{:T(128)}, f32[4,4,128]{2,1,0:T(4,128)S(1)}, f32[4,4,128]{2,1,0:T(4,128)S(1)}, f32[128,4,4,128]{3,0,2,1:T(8,128)S(1)}, bf16[2,128,4,128]{3,1,2...) while((s32[]{:T(128)}, f32[4,4,128]{2,1,0:T(4,128)S(1)}, ...), condition=%wide.region_8.9_spmd.clone, body=%wide.region_2.8_spmd.clone.sunk | while | flops 137124752 | bytes 7803410 | solution.py:187
  18.5 3.3 conditional.8
  21.9 4.9 collective-permute-done
  29.7 3.3 conditional.8
  33.0 5.6 collective-permute-done
  41.5 3.3 conditional.8
  44.9 4.7 collective-permute-done
  52.5 7.7 %collective-permute-done = bf16[2,128,4,128]{3,1,2,0:T(8,128)(2,1)S(1)} collective-permute-done((bf16[2,128,4,128]{3,1,2,0:T(8,128)(2,1)}, bf16[2,128,4,128]{3,1,2,0:T(8,128)(2,1)S(1)}, u32[]{:S(2)}, u32[]{:S(2)}) %collective-permute-start) | collective-permute-done | bytes 262176 | tf_op jit(solution)/shard_map/while/body/eval_jaxpr/ppermute | solution.py:13
  63.1 3.3 conditional.8
  66.4 4.3 collective-permute-done
  73.7 3.3 conditional.8
  77.0 4.3 collective-permute-done
  84.3 3.3 conditional.8
  87.6 4.4 collective-permute-done
  95.0 3.3 conditional.8
  98.3 5.5 collective-permute-done
  106.8 3.3 conditional.8
  110.1 6.7 %collective-permute-done = bf16[2,128,4,128]{3,1,2,0:T(8,128)(2,1)S(1)} collective-permute-done((bf16[2,128,4,128]{3,1,2,0:T(8,128)(2,1)}, bf16[2,128,4,128]{3,1,2,0:T(8,128)(2,1)S(1)}, u32[]{:S(2)}, u32[]{:S(2)}) %collective-permute-start) | collective-permute-done | bytes 262176 | tf_op jit(solution)/shard_map/while/body/eval_jaxpr/ppermute | solution.py:13
  119.8 3.3 conditional.8
  123.2 6.4 %collective-permute-done = bf16[2,128,4,128]{3,1,2,0:T(8,128)(2,1)S(1)} collective-permute-done((bf16[2,128,4,128]{3,1,2,0:T(8,128)(2,1)}, bf16[2,128,4,128]{3,1,2,0:T(8,128)(2,1)S(1)}, u32[]{:S(2)}, u32[]{:S(2)}) %collective-permute-start) | collective-permute-done | bytes 262176 | tf_op jit(solution)/shard_map/while/body/eval_jaxpr/ppermute | solution.py:13
  132.5 3.3 conditional.8
  135.8 5.6 collective-permute-done
  144.3 3.3 conditional.8
  147.7 4.7 collective-permute-done
  155.3 3.3 conditional.8
  158.6 4.3 collective-permute-done
  165.9 3.3 conditional.8
  169.2 4.3 collective-permute-done
  176.5 3.3 conditional.8
  179.8 5.1 collective-permute-done
  192.6 319.1 %while.43 = (s32[]{:T(128)}, f32[128,4,4,128]{3,0,2,1:T(8,128)}, bf16[2,128,4,128]{3,1,2,0:T(8,128)(2,1)S(1)}, f32[2,128,4,128]{3,1,2,0:T(8,128)S(1)}, s32[]{:T(...) while((s32[]{:T(128)}, f32[128,4,4,128]{3,0,2,1:T(8,128)}, ...), condition=%wide.region_18.19_spmd.clone, body=%wide.region_14.0_spmd.clone.sunk | while | flops 338576288 | bytes 17750600 | solution.py:215
  196.0 5.3 conditional.9
  203.3 10.2 %collective-permute-done.2 = bf16[2,128,4,128]{3,1,2,0:T(8,128)(2,1)S(1)} collective-permute-done((bf16[2,128,4,128]{3,1,2,0:T(8,128)(2,1)}, bf16[2,128,4,128]{3,1,2,0:T(8,128)(2,1)S(1)}, u32[]{:S(2)}, u32[]{:S(2)}) %collective-permute-start.2) | collective-permute-done | bytes 262176 | tf_op jit(solution)/shard_map/while/body/eval_jaxpr/ppermute | solution.py:13
  217.0 5.3 conditional.9
  225.4 10.1 %collective-permute-done.2 = bf16[2,128,4,128]{3,1,2,0:T(8,128)(2,1)S(1)} collective-permute-done((bf16[2,128,4,128]{3,1,2,0:T(8,128)(2,1)}, bf16[2,128,4,128]{3,1,2,0:T(8,128)(2,1)S(1)}, u32[]{:S(2)}, u32[]{:S(2)}) %collective-permute-start.2) | collective-permute-done | bytes 262176 | tf_op jit(solution)/shard_map/while/body/eval_jaxpr/ppermute | solution.py:13
  239.1 5.3 conditional.9
  247.5 9.5 %collective-permute-done.2 = bf16[2,128,4,128]{3,1,2,0:T(8,128)(2,1)S(1)} collective-permute-done((bf16[2,128,4,128]{3,1,2,0:T(8,128)(2,1)}, bf16[2,128,4,128]{3,1,2,0:T(8,128)(2,1)S(1)}, u32[]{:S(2)}, u32[]{:S(2)}) %collective-permute-start.2) | collective-permute-done | bytes 262176 | tf_op jit(solution)/shard_map/while/body/eval_jaxpr/ppermute | solution.py:13
  263.8 13.8 %collective-permute-done.2 = bf16[2,128,4,128]{3,1,2,0:T(8,128)(2,1)S(1)} collective-permute-done((bf16[2,128,4,128]{3,1,2,0:T(8,128)(2,1)}, bf16[2,128,4,128]{3,1,2,0:T(8,128)(2,1)S(1)}, u32[]{:S(2)}, u32[]{:S(2)}) %collective-permute-start.2) | collective-permute-done | bytes 262176 | tf_op jit(solution)/shard_map/while/body/eval_jaxpr/ppermute | solution.py:13
  281.1 5.3 conditional.9
  289.6 7.7 %collective-permute-done.2 = bf16[2,128,4,128]{3,1,2,0:T(8,128)(2,1)S(1)} collective-permute-done((bf16[2,128,4,128]{3,1,2,0:T(8,128)(2,1)}, bf16[2,128,4,128]{3,1,2,0:T(8,128)(2,1)S(1)}, u32[]{:S(2)}, u32[]{:S(2)}) %collective-permute-start.2) | collective-permute-done | bytes 262176 | tf_op jit(solution)/shard_map/while/body/eval_jaxpr/ppermute | solution.py:13
  300.8 5.3 conditional.9
  309.2 7.5 %collective-permute-done.2 = bf16[2,128,4,128]{3,1,2,0:T(8,128)(2,1)S(1)} collective-permute-done((bf16[2,128,4,128]{3,1,2,0:T(8,128)(2,1)}, bf16[2,128,4,128]{3,1,2,0:T(8,128)(2,1)S(1)}, u32[]{:S(2)}, u32[]{:S(2)}) %collective-permute-start.2) | collective-permute-done | bytes 262176 | tf_op jit(solution)/shard_map/while/body/eval_jaxpr/ppermute | solution.py:13
  320.3 5.3 conditional.9
  328.7 7.5 %collective-permute-done.2 = bf16[2,128,4,128]{3,1,2,0:T(8,128)(2,1)S(1)} collective-permute-done((bf16[2,128,4,128]{3,1,2,0:T(8,128)(2,1)}, bf16[2,128,4,128]{3,1,2,0:T(8,128)(2,1)S(1)}, u32[]{:S(2)}, u32[]{:S(2)}) %collective-permute-start.2) | collective-permute-done | bytes 262176 | tf_op jit(solution)/shard_map/while/body/eval_jaxpr/ppermute | solution.py:13
  339.7 5.3 conditional.9
  348.2 7.5 %collective-permute-done.2 = bf16[2,128,4,128]{3,1,2,0:T(8,128)(2,1)S(1)} collective-permute-done((bf16[2,128,4,128]{3,1,2,0:T(8,128)(2,1)}, bf16[2,128,4,128]{3,1,2,0:T(8,128)(2,1)S(1)}, u32[]{:S(2)}, u32[]{:S(2)}) %collective-permute-start.2) | collective-permute-done | bytes 262176 | tf_op jit(solution)/shard_map/while/body/eval_jaxpr/ppermute | solution.py:13
  359.2 5.3 conditional.9
  367.7 7.5 %collective-permute-done.2 = bf16[2,128,4,128]{3,1,2,0:T(8,128)(2,1)S(1)} collective-permute-done((bf16[2,128,4,128]{3,1,2,0:T(8,128)(2,1)}, bf16[2,128,4,128]{3,1,2,0:T(8,128)(2,1)S(1)}, u32[]{:S(2)}, u32[]{:S(2)}) %collective-permute-start.2) | collective-permute-done | bytes 262176 | tf_op jit(solution)/shard_map/while/body/eval_jaxpr/ppermute | solution.py:13
  378.7 5.3 conditional.9
  387.2 7.5 %collective-permute-done.2 = bf16[2,128,4,128]{3,1,2,0:T(8,128)(2,1)S(1)} collective-permute-done((bf16[2,128,4,128]{3,1,2,0:T(8,128)(2,1)}, bf16[2,128,4,128]{3,1,2,0:T(8,128)(2,1)S(1)}, u32[]{:S(2)}, u32[]{:S(2)}) %collective-permute-start.2) | collective-permute-done | bytes 262176 | tf_op jit(solution)/shard_map/while/body/eval_jaxpr/ppermute | solution.py:13
  398.2 5.3 conditional.9
  406.6 7.5 %collective-permute-done.2 = bf16[2,128,4,128]{3,1,2,0:T(8,128)(2,1)S(1)} collective-permute-done((bf16[2,128,4,128]{3,1,2,0:T(8,128)(2,1)}, bf16[2,128,4,128]{3,1,2,0:T(8,128)(2,1)S(1)}, u32[]{:S(2)}, u32[]{:S(2)}) %collective-permute-start.2) | collective-permute-done | bytes 262176 | tf_op jit(solution)/shard_map/while/body/eval_jaxpr/ppermute | solution.py:13
  417.6 5.3 conditional.9
  426.1 7.5 %collective-permute-done.2 = bf16[2,128,4,128]{3,1,2,0:T(8,128)(2,1)S(1)} collective-permute-done((bf16[2,128,4,128]{3,1,2,0:T(8,128)(2,1)}, bf16[2,128,4,128]{3,1,2,0:T(8,128)(2,1)S(1)}, u32[]{:S(2)}, u32[]{:S(2)}) %collective-permute-start.2) | collective-permute-done | bytes 262176 | tf_op jit(solution)/shard_map/while/body/eval_jaxpr/ppermute | solution.py:13
  437.1 5.3 conditional.9
  445.6 7.5 %collective-permute-done.2 = bf16[2,128,4,128]{3,1,2,0:T(8,128)(2,1)S(1)} collective-permute-done((bf16[2,128,4,128]{3,1,2,0:T(8,128)(2,1)}, bf16[2,128,4,128]{3,1,2,0:T(8,128)(2,1)S(1)}, u32[]{:S(2)}, u32[]{:S(2)}) %collective-permute-start.2) | collective-permute-done | bytes 262176 | tf_op jit(solution)/shard_map/while/body/eval_jaxpr/ppermute | solution.py:13
  456.6 5.3 conditional.9
  465.1 7.5 %collective-permute-done.2 = bf16[2,128,4,128]{3,1,2,0:T(8,128)(2,1)S(1)} collective-permute-done((bf16[2,128,4,128]{3,1,2,0:T(8,128)(2,1)}, bf16[2,128,4,128]{3,1,2,0:T(8,128)(2,1)S(1)}, u32[]{:S(2)}, u32[]{:S(2)}) %collective-permute-start.2) | collective-permute-done | bytes 262176 | tf_op jit(solution)/shard_map/while/body/eval_jaxpr/ppermute | solution.py:13
  476.1 5.3 conditional.9
  484.5 7.5 %collective-permute-done.2 = bf16[2,128,4,128]{3,1,2,0:T(8,128)(2,1)S(1)} collective-permute-done((bf16[2,128,4,128]{3,1,2,0:T(8,128)(2,1)}, bf16[2,128,4,128]{3,1,2,0:T(8,128)(2,1)S(1)}, u32[]{:S(2)}, u32[]{:S(2)}) %collective-permute-start.2) | collective-permute-done | bytes 262176 | tf_op jit(solution)/shard_map/while/body/eval_jaxpr/ppermute | solution.py:13
  495.6 5.3 conditional.9
  504.0 7.6 %collective-permute-done.2 = bf16[2,128,4,128]{3,1,2,0:T(8,128)(2,1)S(1)} collective-permute-done((bf16[2,128,4,128]{3,1,2,0:T(8,128)(2,1)}, bf16[2,128,4,128]{3,1,2,0:T(8,128)(2,1)S(1)}, u32[]{:S(2)}, u32[]{:S(2)}) %collective-permute-start.2) | collective-permute-done | bytes 262176 | tf_op jit(solution)/shard_map/while/body/eval_jaxpr/ppermute | solution.py:13
  517.6 11.7 %psum.14 = f32[16]{0:T(128)S(1)} all-reduce(f32[16]{0:T(128)S(1)} %convolution_bitcast_fusion.6), channel_id=1, replica_groups=mesh['pipe'=2,'ctx'=16,'dp'=4] {'dp'}, use_global_device_ids=true, to_apply=%region_22.23 | all-reduce | flops 16 | bytes 128 | tf_op jit(solution)/shard_map/psum | solution.py:228
  529.3 35.5 %psum.15 = f32[16]{0:T(128)S(1)} all-reduce(f32[16]{0:T(128)S(1)} %psum.14), channel_id=1, replica_groups=mesh['pipe'=2,'ctx'=16,'dp'=4] {'ctx'}, use_global_device_ids=true, to_apply=%region_23.24 | all-reduce | flops 16 | bytes 128 | tf_op jit(solution)/shard_map/psum | solution.py:228
  (669 shorter events, 268.3 us)
Async XLA Ops:
  0.6 3.7 copy-start
  0.6 10.1 %collective-permute-start.3 = (bf16[1,1,128,2048]{3,2,1,0:T(8,128)(2,1)}, bf16[1,1,128,2048]{3,2,1,0:T(8,128)(2,1)S(1)}, u32[]{:S(2)}, u32[]{:S(2)}) collective-permute-start(bf16[1,1,128,2048]{3,2,1,0:T(8,128)(2,1)} %param.21), channel_id=1, source_target_pairs={{0,64},{64,0},{1,65},{65,1},{2,66},{66,2},{3,67},{67,3},{4,68},{68... | collective-permute-start | bytes 1572872 | tf_op jit(solution)/shard_map/ppermute | solution.py:13
  0.7 3.5 copy-start.18
  2.8 186.3 %collective-permute-start.4 = (bf16[1,1,128,2048]{2,3,1,0:T(8,128)(2,1)}, bf16[1,1,128,2048]{2,3,1,0:T(8,128)(2,1)}, u32[]{:S(2)}, u32[]{:S(2)}) collective-permute-start(bf16[1,1,128,2048]{2,3,1,0:T(8,128)(2,1)} %copy.95), channel_id=1, source_target_pairs={{0,64},{64,0},{1,65},{65,1},{2,66},{66,2},{3,67},{67,3},{4,68},{68... | collective-permute-start | bytes 1572872 | tf_op jit(solution)/shard_map/ppermute | solution.py:13
  6.2 4.9 copy-start.13
  6.8 4.0 copy-start.17
  11.7 1.0 copy-start.8
  13.1 1.0 copy-start.4
  14.7 12.0 %collective-permute-start = (bf16[2,128,4,128]{3,1,2,0:T(8,128)(2,1)}, bf16[2,128,4,128]{3,1,2,0:T(8,128)(2,1)S(1)}, u32[]{:S(2)}, u32[]{:S(2)}) collective-permute-start(bf16[2,128,4,128]{3,1,2,0:T(8,128)(2,1)} %copy.144), channel_id=1, source_target_pairs={{0,4},{4,8},{8,12},{12,16},{16,20},{20,24},{24,28},{28,32},{32,36}... | collective-permute-start | bytes 786440 | tf_op jit(solution)/shard_map/while/body/eval_jaxpr/ppermute | solution.py:13
  27.4 11.2 %collective-permute-start = (bf16[2,128,4,128]{3,1,2,0:T(8,128)(2,1)}, bf16[2,128,4,128]{3,1,2,0:T(8,128)(2,1)S(1)}, u32[]{:S(2)}, u32[]{:S(2)}) collective-permute-start(bf16[2,128,4,128]{3,1,2,0:T(8,128)(2,1)} %copy.144), channel_id=1, source_target_pairs={{0,4},{4,8},{8,12},{12,16},{16,20},{20,24},{24,28},{28,32},{32,36}... | collective-permute-start | bytes 786440 | tf_op jit(solution)/shard_map/while/body/eval_jaxpr/ppermute | solution.py:13
  39.3 10.3 %collective-permute-start = (bf16[2,128,4,128]{3,1,2,0:T(8,128)(2,1)}, bf16[2,128,4,128]{3,1,2,0:T(8,128)(2,1)S(1)}, u32[]{:S(2)}, u32[]{:S(2)}) collective-permute-start(bf16[2,128,4,128]{3,1,2,0:T(8,128)(2,1)} %copy.144), channel_id=1, source_target_pairs={{0,4},{4,8},{8,12},{12,16},{16,20},{20,24},{24,28},{28,32},{32,36}... | collective-permute-start | bytes 786440 | tf_op jit(solution)/shard_map/while/body/eval_jaxpr/ppermute | solution.py:13
  50.2 9.9 %collective-permute-start = (bf16[2,128,4,128]{3,1,2,0:T(8,128)(2,1)}, bf16[2,128,4,128]{3,1,2,0:T(8,128)(2,1)S(1)}, u32[]{:S(2)}, u32[]{:S(2)}) collective-permute-start(bf16[2,128,4,128]{3,1,2,0:T(8,128)(2,1)} %copy.144), channel_id=1, source_target_pairs={{0,4},{4,8},{8,12},{12,16},{16,20},{20,24},{24,28},{28,32},{32,36}... | collective-permute-start | bytes 786440 | tf_op jit(solution)/shard_map/while/body/eval_jaxpr/ppermute | solution.py:13
  60.9 9.9 %collective-permute-start = (bf16[2,128,4,128]{3,1,2,0:T(8,128)(2,1)}, bf16[2,128,4,128]{3,1,2,0:T(8,128)(2,1)S(1)}, u32[]{:S(2)}, u32[]{:S(2)}) collective-permute-start(bf16[2,128,4,128]{3,1,2,0:T(8,128)(2,1)} %copy.144), channel_id=1, source_target_pairs={{0,4},{4,8},{8,12},{12,16},{16,20},{20,24},{24,28},{28,32},{32,36}... | collective-permute-start | bytes 786440 | tf_op jit(solution)/shard_map/while/body/eval_jaxpr/ppermute | solution.py:13
  71.5 9.9 %collective-permute-start = (bf16[2,128,4,128]{3,1,2,0:T(8,128)(2,1)}, bf16[2,128,4,128]{3,1,2,0:T(8,128)(2,1)S(1)}, u32[]{:S(2)}, u32[]{:S(2)}) collective-permute-start(bf16[2,128,4,128]{3,1,2,0:T(8,128)(2,1)} %copy.144), channel_id=1, source_target_pairs={{0,4},{4,8},{8,12},{12,16},{16,20},{20,24},{24,28},{28,32},{32,36}... | collective-permute-start | bytes 786440 | tf_op jit(solution)/shard_map/while/body/eval_jaxpr/ppermute | solution.py:13
  82.1 10.0 %collective-permute-start = (bf16[2,128,4,128]{3,1,2,0:T(8,128)(2,1)}, bf16[2,128,4,128]{3,1,2,0:T(8,128)(2,1)S(1)}, u32[]{:S(2)}, u32[]{:S(2)}) collective-permute-start(bf16[2,128,4,128]{3,1,2,0:T(8,128)(2,1)} %copy.144), channel_id=1, source_target_pairs={{0,4},{4,8},{8,12},{12,16},{16,20},{20,24},{24,28},{28,32},{32,36}... | collective-permute-start | bytes 786440 | tf_op jit(solution)/shard_map/while/body/eval_jaxpr/ppermute | solution.py:13
  92.8 11.1 %collective-permute-start = (bf16[2,128,4,128]{3,1,2,0:T(8,128)(2,1)}, bf16[2,128,4,128]{3,1,2,0:T(8,128)(2,1)S(1)}, u32[]{:S(2)}, u32[]{:S(2)}) collective-permute-start(bf16[2,128,4,128]{3,1,2,0:T(8,128)(2,1)} %copy.144), channel_id=1, source_target_pairs={{0,4},{4,8},{8,12},{12,16},{16,20},{20,24},{24,28},{28,32},{32,36}... | collective-permute-start | bytes 786440 | tf_op jit(solution)/shard_map/while/body/eval_jaxpr/ppermute | solution.py:13
  104.6 12.3 %collective-permute-start = (bf16[2,128,4,128]{3,1,2,0:T(8,128)(2,1)}, bf16[2,128,4,128]{3,1,2,0:T(8,128)(2,1)S(1)}, u32[]{:S(2)}, u32[]{:S(2)}) collective-permute-start(bf16[2,128,4,128]{3,1,2,0:T(8,128)(2,1)} %copy.144), channel_id=1, source_target_pairs={{0,4},{4,8},{8,12},{12,16},{16,20},{20,24},{24,28},{28,32},{32,36}... | collective-permute-start | bytes 786440 | tf_op jit(solution)/shard_map/while/body/eval_jaxpr/ppermute | solution.py:13
  117.6 12.0 %collective-permute-start = (bf16[2,128,4,128]{3,1,2,0:T(8,128)(2,1)}, bf16[2,128,4,128]{3,1,2,0:T(8,128)(2,1)S(1)}, u32[]{:S(2)}, u32[]{:S(2)}) collective-permute-start(bf16[2,128,4,128]{3,1,2,0:T(8,128)(2,1)} %copy.144), channel_id=1, source_target_pairs={{0,4},{4,8},{8,12},{12,16},{16,20},{20,24},{24,28},{28,32},{32,36}... | collective-permute-start | bytes 786440 | tf_op jit(solution)/shard_map/while/body/eval_jaxpr/ppermute | solution.py:13
  130.3 11.1 %collective-permute-start = (bf16[2,128,4,128]{3,1,2,0:T(8,128)(2,1)}, bf16[2,128,4,128]{3,1,2,0:T(8,128)(2,1)S(1)}, u32[]{:S(2)}, u32[]{:S(2)}) collective-permute-start(bf16[2,128,4,128]{3,1,2,0:T(8,128)(2,1)} %copy.144), channel_id=1, source_target_pairs={{0,4},{4,8},{8,12},{12,16},{16,20},{20,24},{24,28},{28,32},{32,36}... | collective-permute-start | bytes 786440 | tf_op jit(solution)/shard_map/while/body/eval_jaxpr/ppermute | solution.py:13
  142.1 10.2 %collective-permute-start = (bf16[2,128,4,128]{3,1,2,0:T(8,128)(2,1)}, bf16[2,128,4,128]{3,1,2,0:T(8,128)(2,1)S(1)}, u32[]{:S(2)}, u32[]{:S(2)}) collective-permute-start(bf16[2,128,4,128]{3,1,2,0:T(8,128)(2,1)} %copy.144), channel_id=1, source_target_pairs={{0,4},{4,8},{8,12},{12,16},{16,20},{20,24},{24,28},{28,32},{32,36}... | collective-permute-start | bytes 786440 | tf_op jit(solution)/shard_map/while/body/eval_jaxpr/ppermute | solution.py:13
  153.0 9.9 %collective-permute-start = (bf16[2,128,4,128]{3,1,2,0:T(8,128)(2,1)}, bf16[2,128,4,128]{3,1,2,0:T(8,128)(2,1)S(1)}, u32[]{:S(2)}, u32[]{:S(2)}) collective-permute-start(bf16[2,128,4,128]{3,1,2,0:T(8,128)(2,1)} %copy.144), channel_id=1, source_target_pairs={{0,4},{4,8},{8,12},{12,16},{16,20},{20,24},{24,28},{28,32},{32,36}... | collective-permute-start | bytes 786440 | tf_op jit(solution)/shard_map/while/body/eval_jaxpr/ppermute | solution.py:13
  163.6 9.9 %collective-permute-start = (bf16[2,128,4,128]{3,1,2,0:T(8,128)(2,1)}, bf16[2,128,4,128]{3,1,2,0:T(8,128)(2,1)S(1)}, u32[]{:S(2)}, u32[]{:S(2)}) collective-permute-start(bf16[2,128,4,128]{3,1,2,0:T(8,128)(2,1)} %copy.144), channel_id=1, source_target_pairs={{0,4},{4,8},{8,12},{12,16},{16,20},{20,24},{24,28},{28,32},{32,36}... | collective-permute-start | bytes 786440 | tf_op jit(solution)/shard_map/while/body/eval_jaxpr/ppermute | solution.py:13
  174.2 10.6 %collective-permute-start = (bf16[2,128,4,128]{3,1,2,0:T(8,128)(2,1)}, bf16[2,128,4,128]{3,1,2,0:T(8,128)(2,1)S(1)}, u32[]{:S(2)}, u32[]{:S(2)}) collective-permute-start(bf16[2,128,4,128]{3,1,2,0:T(8,128)(2,1)} %copy.144), channel_id=1, source_target_pairs={{0,4},{4,8},{8,12},{12,16},{16,20},{20,24},{24,28},{28,32},{32,36}... | collective-permute-start | bytes 786440 | tf_op jit(solution)/shard_map/while/body/eval_jaxpr/ppermute | solution.py:13
  186.5 1.4 copy-start.7
  186.5 1.3 copy-start.9
  189.1 1.4 copy-start.10
  190.5 2.1 copy-start.3
  193.3 20.2 %collective-permute-start.1 = (bf16[2,128,4,128]{3,1,2,0:T(8,128)(2,1)}, bf16[2,128,4,128]{3,1,2,0:T(8,128)(2,1)S(1)}, u32[]{:S(2)}, u32[]{:S(2)}) collective-permute-start(bf16[2,128,4,128]{3,1,2,0:T(8,128)(2,1)} %copy.162), channel_id=1, source_target_pairs={{0,4},{4,8},{8,12},{12,16},{16,20},{20,24},{24,28},{28,32},{32,36}... | collective-permute-start | bytes 786440 | tf_op jit(solution)/shard_map/while/body/eval_jaxpr/ppermute | solution.py:13
  202.1 11.4 %collective-permute-start.2 = (bf16[2,128,4,128]{3,1,2,0:T(8,128)(2,1)}, bf16[2,128,4,128]{3,1,2,0:T(8,128)(2,1)S(1)}, u32[]{:S(2)}, u32[]{:S(2)}) collective-permute-start(bf16[2,128,4,128]{3,1,2,0:T(8,128)(2,1)} %fusion.77), channel_id=1, source_target_pairs={{0,4},{4,8},{8,12},{12,16},{16,20},{20,24},{24,28},{28,32},{32,36}... | collective-permute-start | bytes 786440 | tf_op jit(solution)/shard_map/while/body/eval_jaxpr/ppermute | solution.py:13
  214.3 21.4 %collective-permute-start.1 = (bf16[2,128,4,128]{3,1,2,0:T(8,128)(2,1)}, bf16[2,128,4,128]{3,1,2,0:T(8,128)(2,1)S(1)}, u32[]{:S(2)}, u32[]{:S(2)}) collective-permute-start(bf16[2,128,4,128]{3,1,2,0:T(8,128)(2,1)} %copy.162), channel_id=1, source_target_pairs={{0,4},{4,8},{8,12},{12,16},{16,20},{20,24},{24,28},{28,32},{32,36}... | collective-permute-start | bytes 786440 | tf_op jit(solution)/shard_map/while/body/eval_jaxpr/ppermute | solution.py:13
  223.1 12.5 %collective-permute-start.2 = (bf16[2,128,4,128]{3,1,2,0:T(8,128)(2,1)}, bf16[2,128,4,128]{3,1,2,0:T(8,128)(2,1)S(1)}, u32[]{:S(2)}, u32[]{:S(2)}) collective-permute-start(bf16[2,128,4,128]{3,1,2,0:T(8,128)(2,1)} %fusion.77), channel_id=1, source_target_pairs={{0,4},{4,8},{8,12},{12,16},{16,20},{20,24},{24,28},{28,32},{32,36}... | collective-permute-start | bytes 786440 | tf_op jit(solution)/shard_map/while/body/eval_jaxpr/ppermute | solution.py:13
  236.4 20.7 %collective-permute-start.1 = (bf16[2,128,4,128]{3,1,2,0:T(8,128)(2,1)}, bf16[2,128,4,128]{3,1,2,0:T(8,128)(2,1)S(1)}, u32[]{:S(2)}, u32[]{:S(2)}) collective-permute-start(bf16[2,128,4,128]{3,1,2,0:T(8,128)(2,1)} %copy.162), channel_id=1, source_target_pairs={{0,4},{4,8},{8,12},{12,16},{16,20},{20,24},{24,28},{28,32},{32,36}... | collective-permute-start | bytes 786440 | tf_op jit(solution)/shard_map/while/body/eval_jaxpr/ppermute | solution.py:13
  245.2 11.9 %collective-permute-start.2 = (bf16[2,128,4,128]{3,1,2,0:T(8,128)(2,1)}, bf16[2,128,4,128]{3,1,2,0:T(8,128)(2,1)S(1)}, u32[]{:S(2)}, u32[]{:S(2)}) collective-permute-start(bf16[2,128,4,128]{3,1,2,0:T(8,128)(2,1)} %fusion.77), channel_id=1, source_target_pairs={{0,4},{4,8},{8,12},{12,16},{16,20},{20,24},{24,28},{28,32},{32,36}... | collective-permute-start | bytes 786440 | tf_op jit(solution)/shard_map/while/body/eval_jaxpr/ppermute | solution.py:13
  257.8 19.9 %collective-permute-start.1 = (bf16[2,128,4,128]{3,1,2,0:T(8,128)(2,1)}, bf16[2,128,4,128]{3,1,2,0:T(8,128)(2,1)S(1)}, u32[]{:S(2)}, u32[]{:S(2)}) collective-permute-start(bf16[2,128,4,128]{3,1,2,0:T(8,128)(2,1)} %copy.162), channel_id=1, source_target_pairs={{0,4},{4,8},{8,12},{12,16},{16,20},{20,24},{24,28},{28,32},{32,36}... | collective-permute-start | bytes 786440 | tf_op jit(solution)/shard_map/while/body/eval_jaxpr/ppermute | solution.py:13
  261.4 16.2 %collective-permute-start.2 = (bf16[2,128,4,128]{3,1,2,0:T(8,128)(2,1)}, bf16[2,128,4,128]{3,1,2,0:T(8,128)(2,1)S(1)}, u32[]{:S(2)}, u32[]{:S(2)}) collective-permute-start(bf16[2,128,4,128]{3,1,2,0:T(8,128)(2,1)} %fusion.77), channel_id=1, source_target_pairs={{0,4},{4,8},{8,12},{12,16},{16,20},{20,24},{24,28},{28,32},{32,36}... | collective-permute-start | bytes 786440 | tf_op jit(solution)/shard_map/while/body/eval_jaxpr/ppermute | solution.py:13
  278.4 18.9 %collective-permute-start.1 = (bf16[2,128,4,128]{3,1,2,0:T(8,128)(2,1)}, bf16[2,128,4,128]{3,1,2,0:T(8,128)(2,1)S(1)}, u32[]{:S(2)}, u32[]{:S(2)}) collective-permute-start(bf16[2,128,4,128]{3,1,2,0:T(8,128)(2,1)} %copy.162), channel_id=1, source_target_pairs={{0,4},{4,8},{8,12},{12,16},{16,20},{20,24},{24,28},{28,32},{32,36}... | collective-permute-start | bytes 786440 | tf_op jit(solution)/shard_map/while/body/eval_jaxpr/ppermute | solution.py:13
  287.2 10.1 %collective-permute-start.2 = (bf16[2,128,4,128]{3,1,2,0:T(8,128)(2,1)}, bf16[2,128,4,128]{3,1,2,0:T(8,128)(2,1)S(1)}, u32[]{:S(2)}, u32[]{:S(2)}) collective-permute-start(bf16[2,128,4,128]{3,1,2,0:T(8,128)(2,1)} %fusion.77), channel_id=1, source_target_pairs={{0,4},{4,8},{8,12},{12,16},{16,20},{20,24},{24,28},{28,32},{32,36}... | collective-permute-start | bytes 786440 | tf_op jit(solution)/shard_map/while/body/eval_jaxpr/ppermute | solution.py:13
  298.1 18.7 %collective-permute-start.1 = (bf16[2,128,4,128]{3,1,2,0:T(8,128)(2,1)}, bf16[2,128,4,128]{3,1,2,0:T(8,128)(2,1)S(1)}, u32[]{:S(2)}, u32[]{:S(2)}) collective-permute-start(bf16[2,128,4,128]{3,1,2,0:T(8,128)(2,1)} %copy.162), channel_id=1, source_target_pairs={{0,4},{4,8},{8,12},{12,16},{16,20},{20,24},{24,28},{28,32},{32,36}... | collective-permute-start | bytes 786440 | tf_op jit(solution)/shard_map/while/body/eval_jaxpr/ppermute | solution.py:13
  306.9 9.9 %collective-permute-start.2 = (bf16[2,128,4,128]{3,1,2,0:T(8,128)(2,1)}, bf16[2,128,4,128]{3,1,2,0:T(8,128)(2,1)S(1)}, u32[]{:S(2)}, u32[]{:S(2)}) collective-permute-start(bf16[2,128,4,128]{3,1,2,0:T(8,128)(2,1)} %fusion.77), channel_id=1, source_target_pairs={{0,4},{4,8},{8,12},{12,16},{16,20},{20,24},{24,28},{28,32},{32,36}... | collective-permute-start | bytes 786440 | tf_op jit(solution)/shard_map/while/body/eval_jaxpr/ppermute | solution.py:13
  317.5 18.7 %collective-permute-start.1 = (bf16[2,128,4,128]{3,1,2,0:T(8,128)(2,1)}, bf16[2,128,4,128]{3,1,2,0:T(8,128)(2,1)S(1)}, u32[]{:S(2)}, u32[]{:S(2)}) collective-permute-start(bf16[2,128,4,128]{3,1,2,0:T(8,128)(2,1)} %copy.162), channel_id=1, source_target_pairs={{0,4},{4,8},{8,12},{12,16},{16,20},{20,24},{24,28},{28,32},{32,36}... | collective-permute-start | bytes 786440 | tf_op jit(solution)/shard_map/while/body/eval_jaxpr/ppermute | solution.py:13
  326.3 9.9 %collective-permute-start.2 = (bf16[2,128,4,128]{3,1,2,0:T(8,128)(2,1)}, bf16[2,128,4,128]{3,1,2,0:T(8,128)(2,1)S(1)}, u32[]{:S(2)}, u32[]{:S(2)}) collective-permute-start(bf16[2,128,4,128]{3,1,2,0:T(8,128)(2,1)} %fusion.77), channel_id=1, source_target_pairs={{0,4},{4,8},{8,12},{12,16},{16,20},{20,24},{24,28},{28,32},{32,36}... | collective-permute-start | bytes 786440 | tf_op jit(solution)/shard_map/while/body/eval_jaxpr/ppermute | solution.py:13
  337.0 18.7 %collective-permute-start.1 = (bf16[2,128,4,128]{3,1,2,0:T(8,128)(2,1)}, bf16[2,128,4,128]{3,1,2,0:T(8,128)(2,1)S(1)}, u32[]{:S(2)}, u32[]{:S(2)}) collective-permute-start(bf16[2,128,4,128]{3,1,2,0:T(8,128)(2,1)} %copy.162), channel_id=1, source_target_pairs={{0,4},{4,8},{8,12},{12,16},{16,20},{20,24},{24,28},{28,32},{32,36}... | collective-permute-start | bytes 786440 | tf_op jit(solution)/shard_map/while/body/eval_jaxpr/ppermute | solution.py:13
  345.8 9.9 %collective-permute-start.2 = (bf16[2,128,4,128]{3,1,2,0:T(8,128)(2,1)}, bf16[2,128,4,128]{3,1,2,0:T(8,128)(2,1)S(1)}, u32[]{:S(2)}, u32[]{:S(2)}) collective-permute-start(bf16[2,128,4,128]{3,1,2,0:T(8,128)(2,1)} %fusion.77), channel_id=1, source_target_pairs={{0,4},{4,8},{8,12},{12,16},{16,20},{20,24},{24,28},{28,32},{32,36}... | collective-permute-start | bytes 786440 | tf_op jit(solution)/shard_map/while/body/eval_jaxpr/ppermute | solution.py:13
  356.5 18.7 %collective-permute-start.1 = (bf16[2,128,4,128]{3,1,2,0:T(8,128)(2,1)}, bf16[2,128,4,128]{3,1,2,0:T(8,128)(2,1)S(1)}, u32[]{:S(2)}, u32[]{:S(2)}) collective-permute-start(bf16[2,128,4,128]{3,1,2,0:T(8,128)(2,1)} %copy.162), channel_id=1, source_target_pairs={{0,4},{4,8},{8,12},{12,16},{16,20},{20,24},{24,28},{28,32},{32,36}... | collective-permute-start | bytes 786440 | tf_op jit(solution)/shard_map/while/body/eval_jaxpr/ppermute | solution.py:13
  365.3 9.9 %collective-permute-start.2 = (bf16[2,128,4,128]{3,1,2,0:T(8,128)(2,1)}, bf16[2,128,4,128]{3,1,2,0:T(8,128)(2,1)S(1)}, u32[]{:S(2)}, u32[]{:S(2)}) collective-permute-start(bf16[2,128,4,128]{3,1,2,0:T(8,128)(2,1)} %fusion.77), channel_id=1, source_target_pairs={{0,4},{4,8},{8,12},{12,16},{16,20},{20,24},{24,28},{28,32},{32,36}... | collective-permute-start | bytes 786440 | tf_op jit(solution)/shard_map/while/body/eval_jaxpr/ppermute | solution.py:13
  376.0 18.7 %collective-permute-start.1 = (bf16[2,128,4,128]{3,1,2,0:T(8,128)(2,1)}, bf16[2,128,4,128]{3,1,2,0:T(8,128)(2,1)S(1)}, u32[]{:S(2)}, u32[]{:S(2)}) collective-permute-start(bf16[2,128,4,128]{3,1,2,0:T(8,128)(2,1)} %copy.162), channel_id=1, source_target_pairs={{0,4},{4,8},{8,12},{12,16},{16,20},{20,24},{24,28},{28,32},{32,36}... | collective-permute-start | bytes 786440 | tf_op jit(solution)/shard_map/while/body/eval_jaxpr/ppermute | solution.py:13
  384.8 9.9 %collective-permute-start.2 = (bf16[2,128,4,128]{3,1,2,0:T(8,128)(2,1)}, bf16[2,128,4,128]{3,1,2,0:T(8,128)(2,1)S(1)}, u32[]{:S(2)}, u32[]{:S(2)}) collective-permute-start(bf16[2,128,4,128]{3,1,2,0:T(8,128)(2,1)} %fusion.77), channel_id=1, source_target_pairs={{0,4},{4,8},{8,12},{12,16},{16,20},{20,24},{24,28},{28,32},{32,36}... | collective-permute-start | bytes 786440 | tf_op jit(solution)/shard_map/while/body/eval_jaxpr/ppermute | solution.py:13
  395.4 18.7 %collective-permute-start.1 = (bf16[2,128,4,128]{3,1,2,0:T(8,128)(2,1)}, bf16[2,128,4,128]{3,1,2,0:T(8,128)(2,1)S(1)}, u32[]{:S(2)}, u32[]{:S(2)}) collective-permute-start(bf16[2,128,4,128]{3,1,2,0:T(8,128)(2,1)} %copy.162), channel_id=1, source_target_pairs={{0,4},{4,8},{8,12},{12,16},{16,20},{20,24},{24,28},{28,32},{32,36}... | collective-permute-start | bytes 786440 | tf_op jit(solution)/shard_map/while/body/eval_jaxpr/ppermute | solution.py:13
  404.2 9.9 %collective-permute-start.2 = (bf16[2,128,4,128]{3,1,2,0:T(8,128)(2,1)}, bf16[2,128,4,128]{3,1,2,0:T(8,128)(2,1)S(1)}, u32[]{:S(2)}, u32[]{:S(2)}) collective-permute-start(bf16[2,128,4,128]{3,1,2,0:T(8,128)(2,1)} %fusion.77), channel_id=1, source_target_pairs={{0,4},{4,8},{8,12},{12,16},{16,20},{20,24},{24,28},{28,32},{32,36}... | collective-permute-start | bytes 786440 | tf_op jit(solution)/shard_map/while/body/eval_jaxpr/ppermute | solution.py:13
  414.9 18.7 %collective-permute-start.1 = (bf16[2,128,4,128]{3,1,2,0:T(8,128)(2,1)}, bf16[2,128,4,128]{3,1,2,0:T(8,128)(2,1)S(1)}, u32[]{:S(2)}, u32[]{:S(2)}) collective-permute-start(bf16[2,128,4,128]{3,1,2,0:T(8,128)(2,1)} %copy.162), channel_id=1, source_target_pairs={{0,4},{4,8},{8,12},{12,16},{16,20},{20,24},{24,28},{28,32},{32,36}... | collective-permute-start | bytes 786440 | tf_op jit(solution)/shard_map/while/body/eval_jaxpr/ppermute | solution.py:13
  423.7 9.9 %collective-permute-start.2 = (bf16[2,128,4,128]{3,1,2,0:T(8,128)(2,1)}, bf16[2,128,4,128]{3,1,2,0:T(8,128)(2,1)S(1)}, u32[]{:S(2)}, u32[]{:S(2)}) collective-permute-start(bf16[2,128,4,128]{3,1,2,0:T(8,128)(2,1)} %fusion.77), channel_id=1, source_target_pairs={{0,4},{4,8},{8,12},{12,16},{16,20},{20,24},{24,28},{28,32},{32,36}... | collective-permute-start | bytes 786440 | tf_op jit(solution)/shard_map/while/body/eval_jaxpr/ppermute | solution.py:13
  434.4 18.7 %collective-permute-start.1 = (bf16[2,128,4,128]{3,1,2,0:T(8,128)(2,1)}, bf16[2,128,4,128]{3,1,2,0:T(8,128)(2,1)S(1)}, u32[]{:S(2)}, u32[]{:S(2)}) collective-permute-start(bf16[2,128,4,128]{3,1,2,0:T(8,128)(2,1)} %copy.162), channel_id=1, source_target_pairs={{0,4},{4,8},{8,12},{12,16},{16,20},{20,24},{24,28},{28,32},{32,36}... | collective-permute-start | bytes 786440 | tf_op jit(solution)/shard_map/while/body/eval_jaxpr/ppermute | solution.py:13
  443.2 9.9 %collective-permute-start.2 = (bf16[2,128,4,128]{3,1,2,0:T(8,128)(2,1)}, bf16[2,128,4,128]{3,1,2,0:T(8,128)(2,1)S(1)}, u32[]{:S(2)}, u32[]{:S(2)}) collective-permute-start(bf16[2,128,4,128]{3,1,2,0:T(8,128)(2,1)} %fusion.77), channel_id=1, source_target_pairs={{0,4},{4,8},{8,12},{12,16},{16,20},{20,24},{24,28},{28,32},{32,36}... | collective-permute-start | bytes 786440 | tf_op jit(solution)/shard_map/while/body/eval_jaxpr/ppermute | solution.py:13
  453.9 18.7 %collective-permute-start.1 = (bf16[2,128,4,128]{3,1,2,0:T(8,128)(2,1)}, bf16[2,128,4,128]{3,1,2,0:T(8,128)(2,1)S(1)}, u32[]{:S(2)}, u32[]{:S(2)}) collective-permute-start(bf16[2,128,4,128]{3,1,2,0:T(8,128)(2,1)} %copy.162), channel_id=1, source_target_pairs={{0,4},{4,8},{8,12},{12,16},{16,20},{20,24},{24,28},{28,32},{32,36}... | collective-permute-start | bytes 786440 | tf_op jit(solution)/shard_map/while/body/eval_jaxpr/ppermute | solution.py:13
  462.7 9.9 %collective-permute-start.2 = (bf16[2,128,4,128]{3,1,2,0:T(8,128)(2,1)}, bf16[2,128,4,128]{3,1,2,0:T(8,128)(2,1)S(1)}, u32[]{:S(2)}, u32[]{:S(2)}) collective-permute-start(bf16[2,128,4,128]{3,1,2,0:T(8,128)(2,1)} %fusion.77), channel_id=1, source_target_pairs={{0,4},{4,8},{8,12},{12,16},{16,20},{20,24},{24,28},{28,32},{32,36}... | collective-permute-start | bytes 786440 | tf_op jit(solution)/shard_map/while/body/eval_jaxpr/ppermute | solution.py:13
  473.3 18.7 %collective-permute-start.1 = (bf16[2,128,4,128]{3,1,2,0:T(8,128)(2,1)}, bf16[2,128,4,128]{3,1,2,0:T(8,128)(2,1)S(1)}, u32[]{:S(2)}, u32[]{:S(2)}) collective-permute-start(bf16[2,128,4,128]{3,1,2,0:T(8,128)(2,1)} %copy.162), channel_id=1, source_target_pairs={{0,4},{4,8},{8,12},{12,16},{16,20},{20,24},{24,28},{28,32},{32,36}... | collective-permute-start | bytes 786440 | tf_op jit(solution)/shard_map/while/body/eval_jaxpr/ppermute | solution.py:13
  482.2 9.9 %collective-permute-start.2 = (bf16[2,128,4,128]{3,1,2,0:T(8,128)(2,1)}, bf16[2,128,4,128]{3,1,2,0:T(8,128)(2,1)S(1)}, u32[]{:S(2)}, u32[]{:S(2)}) collective-permute-start(bf16[2,128,4,128]{3,1,2,0:T(8,128)(2,1)} %fusion.77), channel_id=1, source_target_pairs={{0,4},{4,8},{8,12},{12,16},{16,20},{20,24},{24,28},{28,32},{32,36}... | collective-permute-start | bytes 786440 | tf_op jit(solution)/shard_map/while/body/eval_jaxpr/ppermute | solution.py:13
  492.8 18.8 %collective-permute-start.1 = (bf16[2,128,4,128]{3,1,2,0:T(8,128)(2,1)}, bf16[2,128,4,128]{3,1,2,0:T(8,128)(2,1)S(1)}, u32[]{:S(2)}, u32[]{:S(2)}) collective-permute-start(bf16[2,128,4,128]{3,1,2,0:T(8,128)(2,1)} %copy.162), channel_id=1, source_target_pairs={{0,4},{4,8},{8,12},{12,16},{16,20},{20,24},{24,28},{28,32},{32,36}... | collective-permute-start | bytes 786440 | tf_op jit(solution)/shard_map/while/body/eval_jaxpr/ppermute | solution.py:13
  501.6 10.0 %collective-permute-start.2 = (bf16[2,128,4,128]{3,1,2,0:T(8,128)(2,1)}, bf16[2,128,4,128]{3,1,2,0:T(8,128)(2,1)S(1)}, u32[]{:S(2)}, u32[]{:S(2)}) collective-permute-start(bf16[2,128,4,128]{3,1,2,0:T(8,128)(2,1)} %fusion.77), channel_id=1, source_target_pairs={{0,4},{4,8},{8,12},{12,16},{16,20},{20,24},{24,28},{28,32},{32,36}... | collective-permute-start | bytes 786440 | tf_op jit(solution)/shard_map/while/body/eval_jaxpr/ppermute | solution.py:13
  511.7 1.2 copy-start.1
  513.0 1.2 copy-start.5
  513.0 1.2 copy-start.14
  514.2 1.8 copy-start.12
  567.3 1.0 copy-start.11
  (23 other events, 15.8 us)
